TPU v7x, 32 devices: a whole 2x2x4 slice. The times are simulated.
32 devices in a mesh: groups: 2 (over y), band: 4 (over z), mesh: 2 (over x), feat: 2 (over core).
Axes of the slice: x: 2, y: 2, z: 4, core: 2. Of those that a mesh axis runs over, the one named last changes fastest.
Arguments:
- grid_latent: bfloat16 [16384, 512], P(('groups', 'band', 'mesh')), parts along dimension 0, may hold values from -6 to 6
- mesh_latent: bfloat16 [1024, 512], P(('groups', 'band', 'mesh')), parts along dimension 0, may hold values from -6 to 6
- g2m_send: int32 [24576], P(('groups', 'band', 'mesh')), parts along dimension 0, may hold values from 0 to 1023
- g2m_slot: int32 [24576], P(('groups', 'band', 'mesh')), parts along dimension 0, may hold values from 0 to 1535, as said below
- g2m_recv: int32 [24576], P(('groups', 'band', 'mesh')), parts along dimension 0, may hold values from -1 to 63, as said below
- enc_send_w: bfloat16 [512, 512], P(None, 'feat'), may hold values from -0.25 to 0.25
- enc_recv_w: bfloat16 [512, 512], P(None, 'feat'), may hold values from -0.25 to 0.25
- enc_bias: float32 [512], P('feat'), may hold values from -3 to 3
- enc_out_w: bfloat16 [512, 512], P('feat'), may hold values from -0.25 to 0.25
- enc_gain: float32 [512], replicated, may hold values from 0.1 to 1.9
- proc_send: int32 [8192], P(('groups', 'band', 'mesh')), parts along dimension 0, may hold values from 0 to 63
- proc_slot: int32 [8192], P(('groups', 'band', 'mesh')), parts along dimension 0, may hold values from 0 to 511, as said below
- proc_recv: int32 [8192], P(('groups', 'band', 'mesh')), parts along dimension 0, may hold values from -1 to 63, as said below
- proc_send_w: bfloat16 [512, 512], P(None, 'feat'), may hold values from -0.25 to 0.25
- proc_recv_w: bfloat16 [512, 512], P(None, 'feat'), may hold values from -0.25 to 0.25
- proc_bias: float32 [512], P('feat'), may hold values from -3 to 3
- proc_out_w: bfloat16 [512, 512], P('feat'), may hold values from -0.25 to 0.25
- proc_gain: float32 [512], replicated, may hold values from 0.1 to 1.9
- m2g_send: int32 [49152], P(('groups', 'band', 'mesh', 'feat')), parts along dimension 0, may hold values from 0 to 63
- m2g_slot: int32 [49152], P(('groups', 'band', 'mesh', 'feat')), parts along dimension 0, may hold values from 0 to 1535, as said below
- dec_send_w: bfloat16 [512, 512], replicated, may hold values from -0.25 to 0.25
- dec_recv_w: bfloat16 [512, 512], replicated, may hold values from -0.25 to 0.25
- dec_bias: float32 [512], replicated, may hold values from -3 to 3
- dec_out_w: bfloat16 [512, 512], replicated, may hold values from -0.25 to 0.25
- dec_gain: float32 [512], replicated, may hold values from 0.1 to 1.9
Outputs:
- grid_out: bfloat16 [16384, 512], P(('groups', 'band', 'mesh', 'feat')), parts along dimension 0
- mesh_out: bfloat16 [1024, 512], P(('groups', 'band', 'mesh')), parts along dimension 0
There are 2 independent parts, one for each index of `groups`. A program takes and returns all parts, laid end to end along the dimension named above; an argument that names none is the same for every part. Nothing has to cross between parts.
Inputs may be any that keep to these rules, and one draw needn't show every extreme that they name: `g2m_slot`: entry e of shard q names slot (d * 2 + j) * 256 + s: the s-th row that the shard of mesh index j in band (band of q) + d - 1 sends to shard q; that band exists for every live edge. Padding edges hold 0. `g2m_recv`: live edges come first, in ascending order of receiver; every shard has at least one padding edge. `proc_slot`: entry e of shard q names slot p * 64 + s: the s-th row shard p sends to shard q. Padding edges hold 0. `proc_recv`: live edges come first, in ascending order of receiver; every shard has at least one padding edge. `m2g_slot`: entry 3 g + k names slot (d * 2 + j) * 256 + s of the rows sent for grid node g's decoding device by the shard of mesh index j in band (band of g) + d - 1; that band exists.
All inputs are finite; a program needn't handle non-finite values.
Results may differ from a plain program's by a relative error of at most 0.013.
Values may be sent and summed in bfloat16 or wider, within the bound.
A program may use at most 64 MiB of HBM per device.

v0:
```python
import jax
import jax.numpy as jnp
from jax import lax
from jax.sharding import PartitionSpec as P


def shifted(value, axis, steps):
    count = lax.axis_size(axis)
    leading, last = (max(0, -steps), min(count, count - steps))
    return lax.ppermute(value, axis, [(source, source + steps) for source in range(leading, last)])


def layer_norm(values, gain):
    mean = jnp.mean(values, axis=-1, keepdims=True)
    centred = values - mean
    spread = jnp.mean(centred * centred, axis=-1, keepdims=True)
    return centred * lax.rsqrt(spread + 1e-05) * gain


def spread_rows(buffer):
    shards = lax.axis_size("band") * lax.axis_size("mesh")
    width = buffer.shape[1]
    places = buffer.shape[0] // shards
    arrived = lax.all_to_all(
        buffer.reshape(shards, places, width),
        ("band", "mesh"),
        split_axis=0,
        concat_axis=0,
        tiled=True,
    )
    return arrived.reshape(shards * places, width)


def nearby_rows(buffer):
    columns = lax.axis_size("mesh")
    width = buffer.shape[1]
    places = buffer.shape[0] // (3 * columns)
    mixed = lax.all_to_all(
        buffer.reshape(3, columns, places, width), "mesh", split_axis=1, concat_axis=1, tiled=True
    )
    lower = shifted(mixed[0], "band", 1)
    upper = shifted(mixed[2], "band", -1)
    arrived = jnp.stack([lower, mixed[1], upper])
    return arrived.reshape(3 * columns * places, width)


def sender_terms(source, send_list, weight, carry):
    arrived = carry(jnp.take(source, send_list, axis=0))
    return jnp.dot(arrived, weight, preferred_element_type=jnp.float32).astype(jnp.bfloat16)


def aggregate(node_latent, senders, slots, receivers, recv_w, bias, out_w):
    recv_term = jnp.dot(node_latent, recv_w, preferred_element_type=jnp.float32) + bias
    node_rows = node_latent.shape[0]
    local = jnp.maximum(receivers, 0)
    pre = jnp.take(senders, slots, axis=0).astype(jnp.float32) + jnp.take(recv_term, local, axis=0)
    hidden = jax.nn.silu(pre).astype(jnp.bfloat16)
    onehot = (receivers[:, None] == jnp.arange(node_rows, dtype=jnp.int32)[None, :]).astype(
        jnp.bfloat16
    )
    summed = lax.dot_general(
        onehot, hidden, (((0,), (0,)), ((), ())), preferred_element_type=jnp.float32
    )
    return jnp.dot(summed.astype(jnp.bfloat16), out_w, preferred_element_type=jnp.float32)


def per_device(
    grid_latent,
    mesh_latent,
    g2m_send,
    g2m_slot,
    g2m_recv,
    enc_send_w,
    enc_recv_w,
    enc_bias,
    enc_out_w,
    enc_gain,
    proc_send,
    proc_slot,
    proc_recv,
    proc_send_w,
    proc_recv_w,
    proc_bias,
    proc_out_w,
    proc_gain,
    m2g_send,
    m2g_slot,
    dec_send_w,
    dec_recv_w,
    dec_bias,
    dec_out_w,
    dec_gain,
):
    sent = sender_terms(grid_latent, g2m_send, enc_send_w, nearby_rows)
    partial_terms = aggregate(
        mesh_latent, sent, g2m_slot, g2m_recv, enc_recv_w, enc_bias, enc_out_w
    )
    total = lax.psum(partial_terms.astype(jnp.bfloat16), "feat").astype(jnp.float32)
    mesh_first = (mesh_latent.astype(jnp.float32) + layer_norm(total, enc_gain)).astype(
        jnp.bfloat16
    )
    sent = sender_terms(mesh_first, proc_send, proc_send_w, spread_rows)
    partial_terms = aggregate(
        mesh_first, sent, proc_slot, proc_recv, proc_recv_w, proc_bias, proc_out_w
    )
    total = lax.psum(partial_terms.astype(jnp.bfloat16), "feat").astype(jnp.float32)
    mesh_out = (mesh_first.astype(jnp.float32) + layer_norm(total, proc_gain)).astype(jnp.bfloat16)
    sent = sender_terms(mesh_out, m2g_send, dec_send_w, nearby_rows)
    half_rows = grid_latent.shape[0] // lax.axis_size("feat")
    own = lax.dynamic_slice_in_dim(grid_latent, lax.axis_index("feat") * half_rows, half_rows, 0)
    recv_term = jnp.dot(own, dec_recv_w, preferred_element_type=jnp.float32) + dec_bias
    width = own.shape[1]
    pre = (
        jnp.take(sent, m2g_slot, axis=0).reshape(half_rows, 3, width).astype(jnp.float32)
        + recv_term[:, None, :]
    )
    hidden = jax.nn.silu(pre).astype(jnp.bfloat16)
    summed = jnp.sum(hidden, axis=1, dtype=jnp.float32).astype(jnp.bfloat16)
    decoded = jnp.dot(summed, dec_out_w, preferred_element_type=jnp.float32)
    grid_out = (own.astype(jnp.float32) + layer_norm(decoded, dec_gain)).astype(jnp.bfloat16)
    return (grid_out, mesh_out)


def solution(mesh):
    placed = (
        P(("groups", "band", "mesh"), None),
        P(("groups", "band", "mesh"), None),
        P(("groups", "band", "mesh")),
        P(("groups", "band", "mesh")),
        P(("groups", "band", "mesh")),
        P(None, "feat"),
        P(None, "feat"),
        P("feat"),
        P("feat", None),
        P(),
        P(("groups", "band", "mesh")),
        P(("groups", "band", "mesh")),
        P(("groups", "band", "mesh")),
        P(None, "feat"),
        P(None, "feat"),
        P("feat"),
        P("feat", None),
        P(),
        P(("groups", "band", "mesh", "feat")),
        P(("groups", "band", "mesh", "feat")),
        P(),
        P(),
        P(),
        P(),
        P(),
    )
    return jax.shard_map(
        per_device,
        mesh=mesh,
        in_specs=placed,
        out_specs=(
            P(("groups", "band", "mesh", "feat"), None),
            P(("groups", "band", "mesh"), None),
        ),
        check_vma=False,
    )
```

profile of v0, /device:TPU:0, one launch (start us, length us, event | category | flops | bytes accessed | tf_op | source)
XLA Modules:
  0.0 206.9 jit_solution(11583748023558593641)
XLA Ops:
  8.7 4.8 %gather_fusion = bf16[1536,512]{1,0:T(8,128)(2,1)S(1)} fusion(bf16[1024,512]{1,0:T(8,128)(2,1)S(1)} %copy-done, s32[2048]{0:T(1024)S(1)} %pad_clamp_fusion.4), kind=kCustom, calls=%fused_computation | custom fusion | bytes 3151872 | tf_op jit(solution)/shard_map/jit(_take)/gather | solution.py:48
  13.5 1.4 copy_select_fusion.2
  15.0 4.3 %all-to-all-start = ((bf16[3,2,256,512]{3,2,0,1:T(8,128)(2,1)}), bf16[3,2,256,512]{3,2,0,1:T(8,128)(2,1)S(1)}, u32[]{:S(2)}, u32[]{:S(2)}) async-start(bf16[3,2,256,512]{3,2,0,1:T(8,128)(2,1)} %copy_select_fusion.2), calls=%async_computation | async-start | bytes 3145728 | tf_op jit(solution)/shard_map/all_to_all | solution.py:38
  19.7 4.6 %gather_fusion.2 = f32[1536,256]{1,0:T(8,128)} fusion(f32[64,256]{1,0:T(8,128)S(1)} %convolution_add_fusion.2, s32[2048]{0:T(1024)S(1)} %pad_clamp_fusion.2), kind=kCustom, calls=%fused_computation.2 | custom fusion | bytes 3151872 | tf_op jit(solution)/shard_map/jit(_take)/gather | solution.py:56
  24.4 15.1 %all-to-all-done = bf16[3,2,256,512]{3,2,0,1:T(8,128)(2,1)S(1)} async-done(((bf16[3,2,256,512]{3,2,0,1:T(8,128)(2,1)}), bf16[3,2,256,512]{3,2,0,1:T(8,128)(2,1)S(1)}, u32[]{:S(2)}, u32[]{:S(2)}) %all-to-all-start) | async-done | bytes 1572896 | tf_op jit(solution)/shard_map/all_to_all | solution.py:38
  39.6 3.8 %collective-permute-start = (bf16[2,256,512]{2,1,0:T(8,128)(2,1)S(1)}, bf16[2,256,512]{2,1,0:T(8,128)(2,1)S(1)}, u32[]{:S(2)}, u32[]{:S(2)}) collective-permute-start(bf16[2,256,512]{2,1,0:T(8,128)(2,1)S(1)} %get-tuple-element.13), channel_id=1, source_target_pairs={{0,4},{4,8},{8,12},{1,5},{5,9},{9,13},{2,6},{6,10},{10,14},{3,7},{... | collective-permute-start | bytes 1572872 | tf_op jit(solution)/shard_map/ppermute | solution.py:10
  43.4 1.3 collective-permute-start.1
  44.7 8.9 %collective-permute-done = bf16[2,256,512]{2,1,0:T(8,128)(2,1)S(1)} collective-permute-done((bf16[2,256,512]{2,1,0:T(8,128)(2,1)S(1)}, bf16[2,256,512]{2,1,0:T(8,128)(2,1)S(1)}, u32[]{:S(2)}, u32[]{:S(2)}) %collective-permute-start) | collective-permute-done | bytes 524320 | tf_op jit(solution)/shard_map/ppermute | solution.py:10
  53.6 4.1 %collective-permute-done.1 = bf16[2,256,512]{2,1,0:T(8,128)(2,1)S(1)} collective-permute-done((bf16[2,256,512]{2,1,0:T(8,128)(2,1)S(1)}, bf16[2,256,512]{2,1,0:T(8,128)(2,1)S(1)}, u32[]{:S(2)}, u32[]{:S(2)}) %collective-permute-start.1) | collective-permute-done | bytes 524320 | tf_op jit(solution)/shard_map/ppermute | solution.py:10
  59.3 5.4 %gather_fusion.1 = bf16[1536,256]{1,0:T(8,128)(2,1)} fusion(bf16[1536,256]{1,0:T(8,128)(2,1)S(1)} %convolution_convert_fusion.1, s32[2048]{0:T(1024)S(1)} %pad_clamp_fusion.3), kind=kCustom, calls=%fused_computation.1 | custom fusion | bytes 1579008 | tf_op jit(solution)/shard_map/jit(_take)/gather | solution.py:56
  64.7 3.1 %convolution_convert_fusion.4 = bf16[64,512]{1,0:T(8,128)(2,1)} fusion(bf16[256,512]{1,0:T(8,128)(2,1)} %param.33, f32[1536,256]{1,0:T(8,128)S(1)} %copy-done.3, bf16[1536,256]{1,0:T(8,128)(2,1)} %gather_fusion.1, pred[1536]{0:T(1024)(128)(4,1)S(1)} %get-tuple-element.19, pred[1536]{0:T(1024)(128)(4,1)S(1)} %get-tuple-element.18, s32[1536]{0:T(1024)S(1)} %copy-done.14), kind=kOutput, calls=%fused_computation.21 | convolution fusion | flops 70795264 | bytes 2696192 | tf_op jit(solution)/shard_map/dot_general | solution.py:64
  67.8 17.2 %all-reduce.3.cloned.1.call-done = bf16[64,512]{1,0:T(8,128)(2,1)} async-done(((bf16[64,512]{1,0:T(8,128)(2,1)}), bf16[64,512]{1,0:T(8,128)(2,1)}) %all-reduce.3.cloned.1.call-update) | async-done | bytes 65552 | tf_op jit(solution)/shard_map/psum | solution.py:98
  85.9 1.0 fusion.13
  87.9 2.0 gather_fusion.3
  90.9 5.8 %all-to-all-start.1 = ((bf16[8,64,512]{2,1,0:T(8,128)(2,1)}), bf16[8,64,512]{2,1,0:T(8,128)(2,1)S(1)}, u32[]{:S(2)}, u32[]{:S(2)}) async-start(bf16[8,64,512]{2,1,0:T(8,128)(2,1)} %broadcast_select_fusion), calls=%async_computation.1 | async-start | bytes 1048576 | tf_op jit(solution)/shard_map/all_to_all | solution.py:24
  97.0 1.6 gather_fusion.5
  98.6 13.0 %all-to-all-done.1 = bf16[8,64,512]{2,1,0:T(8,128)(2,1)S(1)} async-done(((bf16[8,64,512]{2,1,0:T(8,128)(2,1)}), bf16[8,64,512]{2,1,0:T(8,128)(2,1)S(1)}, u32[]{:S(2)}, u32[]{:S(2)}) %all-to-all-start.1) | async-done | bytes 524320 | tf_op jit(solution)/shard_map/all_to_all | solution.py:24
  111.9 2.0 gather_fusion.4
  113.9 1.2 convolution_convert_fusion.3
  115.2 16.9 %all-reduce.5.cloned.1.call-done = bf16[64,512]{1,0:T(8,128)(2,1)} async-done(((bf16[64,512]{1,0:T(8,128)(2,1)}), bf16[64,512]{1,0:T(8,128)(2,1)}) %all-reduce.5.cloned.1.call-update) | async-done | bytes 65552 | tf_op jit(solution)/shard_map/psum | solution.py:106
  135.0 4.8 %gather_fusion.6 = bf16[1536,512]{1,0:T(8,128)(2,1)S(1)} fusion(bf16[64,512]{1,0:T(8,128)(2,1)S(1)} %fusion.12, s32[2048]{0:T(1024)S(1)} %pad_clamp_fusion.1), kind=kCustom, calls=%fused_computation.6 | custom fusion | bytes 3151872 | tf_op jit(solution)/shard_map/jit(_take)/gather | solution.py:48
  139.9 1.4 copy_select_fusion.1
  141.3 3.8 %all-to-all-start.2 = ((bf16[3,2,256,512]{3,2,0,1:T(8,128)(2,1)}), bf16[3,2,256,512]{3,2,0,1:T(8,128)(2,1)S(1)}, u32[]{:S(2)}, u32[]{:S(2)}) async-start(bf16[3,2,256,512]{3,2,0,1:T(8,128)(2,1)} %copy_select_fusion.1), calls=%async_computation.2 | async-start | bytes 3145728 | tf_op jit(solution)/shard_map/all_to_all | solution.py:38
  146.6 18.4 %all-to-all-done.2 = bf16[3,2,256,512]{3,2,0,1:T(8,128)(2,1)S(1)} async-done(((bf16[3,2,256,512]{3,2,0,1:T(8,128)(2,1)}), bf16[3,2,256,512]{3,2,0,1:T(8,128)(2,1)S(1)}, u32[]{:S(2)}, u32[]{:S(2)}) %all-to-all-start.2) | async-done | bytes 1572896 | tf_op jit(solution)/shard_map/all_to_all | solution.py:38
  165.1 3.8 %collective-permute-start.2 = (bf16[2,256,512]{2,1,0:T(8,128)(2,1)S(1)}, bf16[2,256,512]{2,1,0:T(8,128)(2,1)S(1)}, u32[]{:S(2)}, u32[]{:S(2)}) collective-permute-start(bf16[2,256,512]{2,1,0:T(8,128)(2,1)S(1)} %get-tuple-element.10), channel_id=1, source_target_pairs={{0,4},{4,8},{8,12},{1,5},{5,9},{9,13},{2,6},{6,10},{10,14},{3,7},{... | collective-permute-start | bytes 1572872 | tf_op jit(solution)/shard_map/ppermute | solution.py:10
  169.0 1.5 collective-permute-start.3
  170.5 1.4 convolution_add_fusion
  171.9 7.8 %collective-permute-done.2 = bf16[2,256,512]{2,1,0:T(8,128)(2,1)S(1)} collective-permute-done((bf16[2,256,512]{2,1,0:T(8,128)(2,1)S(1)}, bf16[2,256,512]{2,1,0:T(8,128)(2,1)S(1)}, u32[]{:S(2)}, u32[]{:S(2)}) %collective-permute-start.2) | collective-permute-done | bytes 524320 | tf_op jit(solution)/shard_map/ppermute | solution.py:10
  179.8 4.1 %collective-permute-done.3 = bf16[2,256,512]{2,1,0:T(8,128)(2,1)S(1)} collective-permute-done((bf16[2,256,512]{2,1,0:T(8,128)(2,1)S(1)}, bf16[2,256,512]{2,1,0:T(8,128)(2,1)S(1)}, u32[]{:S(2)}, u32[]{:S(2)}) %collective-permute-start.3) | collective-permute-done | bytes 524320 | tf_op jit(solution)/shard_map/ppermute | solution.py:10
  185.9 5.4 %gather_fusion.7 = bf16[1536,512]{1,0:T(8,128)(2,1)} fusion(bf16[1536,512]{1,0:T(8,128)(2,1)S(1)} %convolution_convert_fusion, s32[2048]{0:T(1024)S(1)} %pad_clamp_fusion), kind=kCustom, calls=%fused_computation.7 | custom fusion | bytes 3151872 | tf_op jit(solution)/shard_map/jit(_take)/gather | solution.py:114
  191.4 4.0 %gather.51 = bf16[512,3,512]{2,1,0:T(4,128)(2,1)S(1)} reshape(bf16[1536,512]{1,0:T(8,128)(2,1)} %gather_fusion.7) | data formatting | bytes 3145728 | tf_op jit(solution)/shard_map/jit(_take)/gather | solution.py:114
  195.4 2.4 %fusion = bf16[512,512]{1,0:T(8,128)(2,1)S(1)} fusion(f32[512,512]{1,0:T(8,128)} %convolution_add_fusion, bf16[512,3,512]{2,1,0:T(4,128)(2,1)S(1)} %gather.51, pred[512,3]{0,1:T(4,128)(4,1)S(1)} %copy.42), kind=kLoop, calls=%fused_computation.17 | loop fusion | flops 6815744 | bytes 3147264 | tf_op jit(solution)/shard_map/reduce_sum | solution.py:118
  (112 shorter events, 15.7 us)
Async XLA Ops:
  7.2 1.5 copy-start
  15.0 4.4 %copy-start.14 = (s32[1536]{0:T(1024)S(1)}, s32[1536]{0:T(1024)}, u32[]{:S(2)}) copy-start(s32[1536]{0:T(1024)} %param.29) | copy-start | bytes 18436
  15.0 4.4 %copy-start.7 = (bf16[512,256]{1,0:T(8,128)(2,1)S(1)}, bf16[512,256]{1,0:T(8,128)(2,1)}, u32[]{:S(2)}) copy-start(bf16[512,256]{1,0:T(8,128)(2,1)} %param.31) | copy-start | bytes 786436
  15.0 4.4 %copy-start.9 = (bf16[64,512]{1,0:T(8,128)(2,1)S(1)}, bf16[64,512]{1,0:T(8,128)(2,1)}, u32[]{:S(2)}) copy-start(bf16[64,512]{1,0:T(8,128)(2,1)} %param.26) | copy-start | bytes 196612
  15.0 4.4 %copy-start.22 = (f32[256]{0:T(256)S(1)}, f32[256]{0:T(256)}, u32[]{:S(2)}) copy-start(f32[256]{0:T(256)} %param.32) | copy-start | bytes 3076
  15.0 4.6 %copy-start.15 = (s32[512]{0:T(512)S(1)}, s32[512]{0:T(512)}, u32[]{:S(2)}) copy-start(s32[512]{0:T(512)} %param.35) | copy-start | bytes 6148
  15.0 24.5 %all-to-all-start = ((bf16[3,2,256,512]{3,2,0,1:T(8,128)(2,1)}), bf16[3,2,256,512]{3,2,0,1:T(8,128)(2,1)S(1)}, u32[]{:S(2)}, u32[]{:S(2)}) async-start(bf16[3,2,256,512]{3,2,0,1:T(8,128)(2,1)} %copy_select_fusion.2), calls=%async_computation | async-start | bytes 3145728 | tf_op jit(solution)/shard_map/all_to_all | solution.py:38
  19.3 65.6 %all-reduce.3.cloned.1.call-start = ((), (), s32[]{:S(2)}) async-start(), calls=%async_computation.3 | async-start | bytes 131072 | tf_op jit(solution)/shard_map/psum | solution.py:98
  19.7 4.7 %copy-start.16 = (s32[512]{0:T(512)S(1)}, s32[512]{0:T(512)}, u32[]{:S(2)}) copy-start(s32[512]{0:T(512)} %param.36) | copy-start | bytes 6148
  19.7 4.7 %copy-start.13 = (s32[1536]{0:T(1024)S(1)}, s32[1536]{0:T(1024)}, u32[]{:S(2)}) copy-start(s32[1536]{0:T(1024)} %param.28) | copy-start | bytes 18436
  24.4 20.3 %copy-start.11 = (s32[1536]{0:T(1024)S(1)}, s32[1536]{0:T(1024)}, u32[]{:S(2)}) copy-start(s32[1536]{0:T(1024)} %param.43) | copy-start | bytes 18436
  39.6 14.0 %collective-permute-start = (bf16[2,256,512]{2,1,0:T(8,128)(2,1)S(1)}, bf16[2,256,512]{2,1,0:T(8,128)(2,1)S(1)}, u32[]{:S(2)}, u32[]{:S(2)}) collective-permute-start(bf16[2,256,512]{2,1,0:T(8,128)(2,1)S(1)} %get-tuple-element.13), channel_id=1, source_target_pairs={{0,4},{4,8},{8,12},{1,5},{5,9},{9,13},{2,6},{6,10},{10,14},{3,7},{... | collective-permute-start | bytes 1572872 | tf_op jit(solution)/shard_map/ppermute | solution.py:10
  43.4 14.4 %collective-permute-start.1 = (bf16[2,256,512]{2,1,0:T(8,128)(2,1)S(1)}, bf16[2,256,512]{2,1,0:T(8,128)(2,1)S(1)}, u32[]{:S(2)}, u32[]{:S(2)}) collective-permute-start(bf16[2,256,512]{2,1,0:T(8,128)(2,1)S(1)} %get-tuple-element.14), channel_id=1, source_target_pairs={{4,0},{8,4},{12,8},{5,1},{9,5},{13,9},{6,2},{10,6},{14,10},{7,3},{... | collective-permute-start | bytes 1572872 | tf_op jit(solution)/shard_map/ppermute | solution.py:10
  59.3 5.4 %copy-start.3 = (f32[1536,256]{1,0:T(8,128)S(1)}, f32[1536,256]{1,0:T(8,128)}, u32[]{:S(2)}) copy-start(f32[1536,256]{1,0:T(8,128)} %gather_fusion.2) | copy-start | bytes 4718596
  64.7 22.3 %copy-start.18 = (f32[512]{0:T(512)S(1)}, f32[512]{0:T(512)}, u32[]{:S(2)}) copy-start(f32[512]{0:T(512)} %param.34) | copy-start | bytes 6148
  89.9 6.8 %copy-start.17 = (s32[512]{0:T(512)S(1)}, s32[512]{0:T(512)}, u32[]{:S(2)}) copy-start(s32[512]{0:T(512)} %param.37) | copy-start | bytes 6148
  89.9 6.9 %copy-start.8 = (bf16[512,256]{1,0:T(8,128)(2,1)S(1)}, bf16[512,256]{1,0:T(8,128)(2,1)}, u32[]{:S(2)}) copy-start(bf16[512,256]{1,0:T(8,128)(2,1)} %param.39) | copy-start | bytes 786436
  89.9 6.9 %copy-start.23 = (f32[256]{0:T(256)S(1)}, f32[256]{0:T(256)}, u32[]{:S(2)}) copy-start(f32[256]{0:T(256)} %param.40) | copy-start | bytes 3076
  90.9 20.7 %all-to-all-start.1 = ((bf16[8,64,512]{2,1,0:T(8,128)(2,1)}), bf16[8,64,512]{2,1,0:T(8,128)(2,1)S(1)}, u32[]{:S(2)}, u32[]{:S(2)}) async-start(bf16[8,64,512]{2,1,0:T(8,128)(2,1)} %broadcast_select_fusion), calls=%async_computation.1 | async-start | bytes 1048576 | tf_op jit(solution)/shard_map/all_to_all | solution.py:24
  96.6 35.4 %all-reduce.5.cloned.1.call-start = ((), (), s32[]{:S(2)}) async-start(), calls=%async_computation.4 | async-start | bytes 131072 | tf_op jit(solution)/shard_map/psum | solution.py:106
  97.0 14.6 %copy-start.10 = (bf16[512,256]{1,0:T(8,128)(2,1)S(1)}, bf16[512,256]{1,0:T(8,128)(2,1)}, u32[]{:S(2)}) copy-start(bf16[512,256]{1,0:T(8,128)(2,1)} %param.38) | copy-start | bytes 786436
  111.6 2.3 %copy-start.25 = (bf16[256,512]{1,0:T(8,128)(2,1)S(1)}, bf16[256,512]{1,0:T(8,128)(2,1)}, u32[]{:S(2)}) copy-start(bf16[256,512]{1,0:T(8,128)(2,1)} %param.41) | copy-start | bytes 786436
  113.9 20.2 %copy-start.19 = (f32[512]{0:T(512)S(1)}, f32[512]{0:T(512)}, u32[]{:S(2)}) copy-start(f32[512]{0:T(512)} %param.42) | copy-start | bytes 6148
  135.0 4.8 %copy-start.1 = (bf16[64,512]{1,0:T(8,128)(2,1)}, bf16[64,512]{1,0:T(8,128)(2,1)S(1)}, u32[]{:S(2)}) copy-start(bf16[64,512]{1,0:T(8,128)(2,1)S(1)} %fusion.12) | copy-start | bytes 196612
  141.3 3.8 %copy-start.12 = (s32[1536]{0:T(1024)S(1)}, s32[1536]{0:T(1024)}, u32[]{:S(2)}) copy-start(s32[1536]{0:T(1024)} %param.44) | copy-start | bytes 18436
  141.3 23.7 %all-to-all-start.2 = ((bf16[3,2,256,512]{3,2,0,1:T(8,128)(2,1)}), bf16[3,2,256,512]{3,2,0,1:T(8,128)(2,1)S(1)}, u32[]{:S(2)}, u32[]{:S(2)}) async-start(bf16[3,2,256,512]{3,2,0,1:T(8,128)(2,1)} %copy_select_fusion.1), calls=%async_computation.2 | async-start | bytes 3145728 | tf_op jit(solution)/shard_map/all_to_all | solution.py:38
  146.6 23.9 %copy-start.20 = (f32[512]{0:T(512)S(1)}, f32[512]{0:T(512)}, u32[]{:S(2)}) copy-start(f32[512]{0:T(512)} %param.47) | copy-start | bytes 6148
  165.0 5.5 %copy-start.4 = (bf16[512,512]{1,0:T(8,128)(2,1)S(1)}, bf16[512,512]{1,0:T(8,128)(2,1)}, u32[]{:S(2)}) copy-start(bf16[512,512]{1,0:T(8,128)(2,1)} %param.46) | copy-start | bytes 1572868
  165.1 14.6 %collective-permute-start.2 = (bf16[2,256,512]{2,1,0:T(8,128)(2,1)S(1)}, bf16[2,256,512]{2,1,0:T(8,128)(2,1)S(1)}, u32[]{:S(2)}, u32[]{:S(2)}) collective-permute-start(bf16[2,256,512]{2,1,0:T(8,128)(2,1)S(1)} %get-tuple-element.10), channel_id=1, source_target_pairs={{0,4},{4,8},{8,12},{1,5},{5,9},{9,13},{2,6},{6,10},{10,14},{3,7},{... | collective-permute-start | bytes 1572872 | tf_op jit(solution)/shard_map/ppermute | solution.py:10
  169.0 14.9 %collective-permute-start.3 = (bf16[2,256,512]{2,1,0:T(8,128)(2,1)S(1)}, bf16[2,256,512]{2,1,0:T(8,128)(2,1)S(1)}, u32[]{:S(2)}, u32[]{:S(2)}) collective-permute-start(bf16[2,256,512]{2,1,0:T(8,128)(2,1)S(1)} %get-tuple-element.11), channel_id=1, source_target_pairs={{4,0},{8,4},{12,8},{5,1},{9,5},{13,9},{6,2},{10,6},{14,10},{7,3},{... | collective-permute-start | bytes 1572872 | tf_op jit(solution)/shard_map/ppermute | solution.py:10
  195.4 2.4 %copy-start.5 = (bf16[512,512]{1,0:T(8,128)(2,1)S(1)}, bf16[512,512]{1,0:T(8,128)(2,1)}, u32[]{:S(2)}) copy-start(bf16[512,512]{1,0:T(8,128)(2,1)} %param.48) | copy-start | bytes 1572868
  197.8 1.0 copy-start.2
  (3 other events, 3.0 us)
Sparse Core Ops, SparseCore 0:
  67.9 17.0 all-reduce.2
  115.3 16.7 all-reduce.4
where the time goes:
time: 208 us; the launch traced here: 207 us
  waiting for transfers between devices  106 us (51%)
  local copies, waits for them, and re-layouts  39.4 us (19%)
  starting transfers between devices  24.3 us (12%)
  between operations  14.7 us (7%)
  other arithmetic  14.4 us (7%)
  matrix products  8.45 us (4%)
    psum x2, waiting for transfers between devices, per_device(): lax.psum(partial_terms.astype(jnp.bfloat16), 'feat').astype(jnp.float32)  34.1 us
    all_to_all x2, waiting for transfers between devices, nearby_rows(): lax.all_to_all(buffer.reshape(3, columns, places, width), 'mesh', split_a...  33.5 us
    ppermute x4, waiting for transfers between devices, shifted(): lax.ppermute(value, axis, [(source, source + steps) for source in range(l...  25 us
    all_to_all x1, waiting for transfers between devices, spread_rows(): lax.all_to_all(buffer.reshape(shards, places, width), ('band', 'mesh'), s...  13 us
    gather x3, local copies, waits for them, and re-layouts, sender_terms(): arrived = carry(jnp.take(source, send_list, axis=0))  11.6 us
    ppermute x4, starting transfers between devices, shifted(): lax.ppermute(value, axis, [(source, source + steps) for source in range(l...  10.4 us
    gather x2, local copies, waits for them, and re-layouts, per_device(): jnp.take(sent, m2g_slot, axis=0).reshape(half_rows, 3, width)  9.41 us
    all_to_all x2, starting transfers between devices, nearby_rows(): lax.all_to_all(buffer.reshape(3, columns, places, width), 'mesh', split_a...  8.15 us
  transfers between devices with their start and end apart: 9, of which 9 were waited for; matrix products, arithmetic and copies ran while one was open for 5% of the time, Pallas kernels for 0%

commit v1 on v0

v1 whole, which is shorter than its diff:
```python
import functools

import jax
import jax.numpy as jnp
from jax import lax
from jax.experimental import pallas as pl
from jax.experimental.pallas import tpu as pltpu
from jax.sharding import PartitionSpec as P

MESH = pl.DeviceIdType.MESH
LANES = 128
BF = jnp.bfloat16
F32 = jnp.float32


def dot(a, b):
    return jnp.dot(a, b, preferred_element_type=F32)


def normed(values, gain):
    mean = jnp.mean(values, axis=-1, keepdims=True)
    centred = values - mean
    spread = jnp.mean(centred * centred, axis=-1, keepdims=True)
    return centred * lax.rsqrt(spread + 1e-05) * gain


def silu(x):
    half = 0.5 * x
    return half + half * jnp.tanh(half)


def columns(row):
    return jnp.transpose(jnp.broadcast_to(row, (LANES, row.shape[1])))


def pick(cols, width):
    lane = lax.broadcasted_iota(jnp.int32, cols.shape, 1)
    if width < LANES:
        cols, lane = cols[:, :width], lane[:, :width]
        return jnp.where(cols == lane, 1.0, 0.0).astype(BF)
    parts = [
        jnp.where(cols == lane + t * LANES, 1.0, 0.0).astype(BF) for t in range(width // LANES)
    ]
    return parts[0] if len(parts) == 1 else jnp.concatenate(parts, axis=1)


def kernel(
    nb, nm, cap_g, cap_h, cap_m,
    grid_ref, mesh_ref, g_send, g_slot, g_recv, e_sw, e_rw, e_b, e_ow, e_g,
    p_send, p_slot, p_recv, p_sw, p_rw, p_b, p_ow, p_g,
    m_send, m_slot, d_sw, d_rw, d_b, d_ow, d_g,
    grid_out, mesh_out,
    gp, ebuf, erecv, ecol, hid, hid2, own_term, pbuf, precv, iref, dcol, dproj, dtab,
    part, other,
    es, er, is_, ir, ps, pr, ds, dr, fs, fr,
):
    shards = nb * nm
    band, col, feat = lax.axis_index("band"), lax.axis_index("mesh"), lax.axis_index("feat")
    me = band * nm + col
    mrows = mesh_ref.shape[0]
    half = grid_out.shape[0]
    dh = e_sw.shape[1]
    near = 3 * nm

    def at_shard(shard):
        return {"band": shard // nm, "mesh": lax.rem(shard, nm)}

    barrier = pltpu.get_barrier_semaphore()
    for o in range(1, shards):
        peer = lax.rem(me + o, shards)
        pl.semaphore_signal(barrier, inc=1, device_id=at_shard(peer), device_id_type=MESH)
    pl.semaphore_signal(barrier, inc=1, device_id={"feat": 1 - feat}, device_id_type=MESH)

    gp[...] = dot(grid_ref[...], e_sw[...]).astype(BF)
    for d, edge in ((0, 0), (2, nb - 1)):
        @pl.when(band == edge)
        def _(d=d):
            for j in range(nm):
                i = d * nm + j
                erecv[i] = jnp.zeros(erecv.shape[1:], BF)
                iref[i] = jnp.zeros(iref.shape[1:], jnp.int32)
                dtab[i] = jnp.zeros(dtab.shape[1:], BF)

    pl.semaphore_wait(barrier, shards)

    def near_copy(src, dst, send, recv, d, o):
        to = lax.rem(col + o, nm)
        return pltpu.make_async_remote_copy(
            src_ref=src(d * nm + to),
            dst_ref=dst.at[d * nm + col],
            send_sem=send.at[d * nm + o],
            recv_sem=recv.at[d * nm + col],
            device_id={"band": band + 1 - d, "mesh": to},
            device_id_type=MESH,
        )

    def near_arrival(dst, send, recv, d, o):
        source = lax.rem(col + o, nm)
        return pltpu.make_async_remote_copy(
            src_ref=dst.at[d * nm + source],
            dst_ref=dst.at[d * nm + source],
            send_sem=send.at[d * nm + o],
            recv_sem=recv.at[d * nm + source],
            device_id={"band": band + d - 1, "mesh": source},
            device_id_type=MESH,
        )

    def to_there(d):
        return {0: band + 1 < nb, 2: band > 0, 1: None}[d]

    def from_there(d):
        return {0: band > 0, 2: band + 1 < nb, 1: None}[d]

    def when(cond, f):
        if cond is None:
            f()
        else:
            pl.when(cond)(f)

    order = [(d, o) for d in (0, 2, 1) for o in reversed(range(nm)) if (d, o) != (1, 0)]

    for d, o in order:
        when(to_there(d), lambda d=d, o=o: near_copy(lambda i: m_send.at[i], iref, is_, ir, d, o).start())
    iref[nm + col] = m_send[nm + col]

    def gathered(i):
        return dot(pick(columns(g_send[i]), gp.shape[0]), gp[...]).astype(BF)

    for d, o in order:
        def send(d=d, o=o):
            i = d * nm + lax.rem(col + o, nm)
            ebuf[i] = gathered(i)
            near_copy(lambda i: ebuf.at[i], erecv, es, er, d, o).start()
        when(to_there(d), send)
    erecv[nm + col] = gathered(nm + col)

    own = pl.ds(pl.multiple_of(feat * half, half), half)
    own_term[...] = dot(grid_ref[own, :], d_rw[...]) + d_b[...]

    def split_term(values, weight, bias):
        term = dot(values, weight[...]) + bias[...]
        high = term.astype(BF)
        return jnp.concatenate([high, (term - high.astype(F32)).astype(BF)], axis=0)

    def pick2(cols):
        lane = lax.broadcasted_iota(jnp.int32, cols.shape, 1)
        if 2 * mrows == LANES:
            lane = jnp.where(lane >= mrows, lane - mrows, lane)
            return jnp.where(cols == lane, 1.0, 0.0).astype(BF)
        single = pick(cols, mrows)
        return jnp.concatenate([single, single], axis=1)

    eterm = split_term(mesh_ref[...], e_rw, e_b)

    for d, o in order:
        when(from_there(d), lambda d=d, o=o: near_arrival(iref, is_, ir, d, o).wait_recv())
    nedge = m_slot.shape[0] * m_slot.shape[2]
    tables = [columns(iref[i]).astype(F32).astype(BF) for i in range(near)]
    for k in range(3):
        slots = columns(m_slot[k])
        block = jnp.zeros(slots.shape, jnp.int32)
        row = jnp.zeros(slots.shape, F32)
        for i in range(near):
            row = row + dot(pick(slots - i * cap_m, cap_m), tables[i])
            if i:
                block = block + jnp.where(slots >= i * cap_m, mrows, 0)
        dcol[pl.ds(k * half, half), :] = block + (row + 0.5).astype(jnp.int32)

    ecol[0] = columns(g_slot[...])
    ecol[1] = columns(g_recv[...])
    for d, o in order:
        when(from_there(d), lambda d=d, o=o: near_arrival(erecv, es, er, d, o).wait_recv())
    chunk = 256

    def edges(c, carry):
        rows = pl.ds(pl.multiple_of(c * chunk, chunk), chunk)
        pre = dot(pick(ecol[0, rows, :], near * cap_g), erecv[...].reshape(near * cap_g, dh))
        pre = pre.astype(BF).astype(F32) + dot(pick2(ecol[1, rows, :]), eterm)
        hid[rows, :] = silu(pre).astype(BF)
        return carry

    lax.fori_loop(0, hid.shape[0] // chunk, edges, 0)

    def finish(base, recv, hidden, ow, gain, n):
        place = lax.broadcasted_iota(jnp.int32, (mrows, recv.shape[1]), 0)
        onto = jnp.where(recv[...] == place, 1.0, 0.0).astype(BF)
        summed = dot(onto, hidden[...]).astype(BF)
        part[n] = dot(summed, ow[...]).astype(BF)
        copy = pltpu.make_async_remote_copy(
            src_ref=part.at[n], dst_ref=other.at[n], send_sem=fs.at[n], recv_sem=fr.at[n],
            device_id={"feat": 1 - feat}, device_id_type=MESH,
        )
        copy.start()
        copy.wait()
        total = part[n].astype(F32) + other[n].astype(F32)
        return (base.astype(F32) + normed(total, gain[...])).astype(BF)

    psend_pick = pick(columns(p_send[...]), mrows)
    pslot_pick = pick(columns(p_slot[...]), shards * cap_h)
    precv_pick = pick2(columns(p_recv[...]))
    first = finish(mesh_ref[...], g_recv, hid, e_ow, e_g, 0)

    mproj = dot(first, p_sw[...]).astype(BF)
    pbuf[...] = dot(psend_pick, mproj).astype(BF).reshape(pbuf.shape)

    def proc_copy(o):
        peer = lax.rem(me + o, shards)
        return pltpu.make_async_remote_copy(
            src_ref=pbuf.at[peer], dst_ref=precv.at[me], send_sem=ps.at[o], recv_sem=pr.at[me],
            device_id=at_shard(peer), device_id_type=MESH,
        )

    def proc_arrival(o):
        peer = lax.rem(me + o, shards)
        return pltpu.make_async_remote_copy(
            src_ref=precv.at[peer], dst_ref=precv.at[peer], send_sem=ps.at[o],
            recv_sem=pr.at[peer], device_id=at_shard(peer), device_id_type=MESH,
        )

    for o in range(1, shards):
        proc_copy(o).start()
    precv[me] = pbuf[me]
    pterm = dot(precv_pick, split_term(first, p_rw, p_b))
    for o in range(1, shards):
        proc_arrival(o).wait_recv()
    pre = dot(pslot_pick, precv[...].reshape(shards * cap_h, dh)) + pterm
    hid2[...] = silu(pre).astype(BF)
    last = finish(first, p_recv, hid2, p_ow, p_g, 1)
    mesh_out[...] = last

    projected = dot(last, d_sw[...]).astype(BF)
    dproj[...] = projected
    for d, o in order:
        when(to_there(d), lambda d=d, o=o: near_copy(lambda i: dproj, dtab, ds, dr, d, o).start())
    dtab[nm + col] = projected
    for d, o in order:
        when(from_there(d), lambda d=d, o=o: near_arrival(dtab, ds, dr, d, o).wait_recv())
    dchunk = 128

    def decode(c, carry):
        rows = pl.ds(pl.multiple_of(c * dchunk, dchunk), dchunk)
        term = own_term[rows, :]
        table = dtab[...].reshape(near * mrows, dtab.shape[2])
        summed = jnp.zeros(term.shape, F32)
        for k in range(3):
            idx = dcol[pl.ds(pl.multiple_of(k * half + c * dchunk, dchunk), dchunk), :]
            pre = dot(pick(idx, near * mrows), table) + term
            summed = summed + silu(pre).astype(BF).astype(F32)
        decoded = dot(summed.astype(BF), d_ow[...])
        base = grid_ref[pl.ds(pl.multiple_of(feat * half + c * dchunk, dchunk), dchunk), :]
        grid_out[rows, :] = (base.astype(F32) + normed(decoded, d_g[...])).astype(BF)
        return carry

    lax.fori_loop(0, half // dchunk, decode, 0)

    for d, o in order:
        def done(d=d, o=o):
            near_copy(lambda i: m_send.at[i], iref, is_, ir, d, o).wait_send()
            near_copy(lambda i: ebuf.at[i], erecv, es, er, d, o).wait_send()
            near_copy(lambda i: dproj, dtab, ds, dr, d, o).wait_send()
        when(to_there(d), done)
    for o in range(1, shards):
        proc_copy(o).wait_send()


def per_device(
    grid_latent, mesh_latent,
    g2m_send, g2m_slot, g2m_recv, enc_send_w, enc_recv_w, enc_bias, enc_out_w, enc_gain,
    proc_send, proc_slot, proc_recv, proc_send_w, proc_recv_w, proc_bias, proc_out_w, proc_gain,
    m2g_send, m2g_slot, dec_send_w, dec_recv_w, dec_bias, dec_out_w, dec_gain,
):
    nb, nm = lax.axis_size("band"), lax.axis_size("mesh")
    shards, near = nb * nm, 3 * nm
    rows, width = grid_latent.shape
    mrows = mesh_latent.shape[0]
    half = rows // lax.axis_size("feat")
    dh = enc_send_w.shape[1]
    cap_g = g2m_send.shape[0] // near
    cap_m = m2g_send.shape[0] // near
    cap_h = proc_send.shape[0] // shards
    if cap_h % 16:
        padded = -(-cap_h // 16) * 16
        proc_send = jnp.pad(proc_send.reshape(shards, cap_h), ((0, 0), (0, padded - cap_h)))
        proc_slot = proc_slot // cap_h * padded + proc_slot % cap_h
        cap_h = padded
    row = lambda v: v.reshape(1, -1)
    args = (
        grid_latent, mesh_latent,
        g2m_send.reshape(near, 1, cap_g), row(g2m_slot), row(g2m_recv),
        enc_send_w, enc_recv_w, row(enc_bias), enc_out_w, row(enc_gain),
        row(proc_send), row(proc_slot), row(proc_recv),
        proc_send_w, proc_recv_w, row(proc_bias), proc_out_w, row(proc_gain),
        m2g_send.reshape(near, 1, cap_m), m2g_slot.reshape(half, 3).T.reshape(3, 1, half),
        dec_send_w, dec_recv_w, row(dec_bias), dec_out_w, row(dec_gain),
    )
    vmem = pl.BlockSpec(memory_space=pltpu.VMEM)
    dma = pltpu.SemaphoreType.DMA
    scratch = [
        pltpu.VMEM((rows, dh), BF),
        pltpu.VMEM((near, cap_g, dh), BF),
        pltpu.VMEM((near, cap_g, dh), BF),
        pltpu.VMEM((2, g2m_slot.shape[0], LANES), jnp.int32),
        pltpu.VMEM((g2m_slot.shape[0], dh), BF),
        pltpu.VMEM((proc_slot.shape[0], dh), BF),
        pltpu.VMEM((half, width), F32),
        pltpu.VMEM((shards, cap_h, dh), BF),
        pltpu.VMEM((shards, cap_h, dh), BF),
        pltpu.VMEM((near, 1, cap_m), jnp.int32),
        pltpu.VMEM((3 * half, LANES), jnp.int32),
        pltpu.VMEM((mrows, width), BF),
        pltpu.VMEM((near, mrows, width), BF),
        pltpu.VMEM((2, mrows, width), BF),
        pltpu.VMEM((2, mrows, width), BF),
        dma((near,)), dma((near,)), dma((near,)), dma((near,)),
        dma((shards,)), dma((shards,)), dma((near,)), dma((near,)),
        dma((2,)), dma((2,)),
    ]
    grid_out, mesh_out = pl.pallas_call(
        functools.partial(kernel, nb, nm, cap_g, cap_h, cap_m),
        out_shape=(
            jax.ShapeDtypeStruct((half, width), BF),
            jax.ShapeDtypeStruct((mrows, width), BF),
        ),
        in_specs=[vmem] * len(args),
        out_specs=(vmem, vmem),
        scratch_shapes=scratch,
        compiler_params=pltpu.CompilerParams(
            collective_id=0, has_side_effects=True, vmem_limit_bytes=48 * 1024 * 1024
        ),
    )(*args)
    return (grid_out, mesh_out)


def solution(mesh):
    shard = P(("groups", "band", "mesh"))
    rows = P(("groups", "band", "mesh"), None)
    finer = P(("groups", "band", "mesh", "feat"))
    layer = (P(None, "feat"), P(None, "feat"), P("feat"), P("feat", None), P())
    return jax.shard_map(
        per_device,
        mesh=mesh,
        in_specs=(rows, rows, shard, shard, shard, *layer, shard, shard, shard, *layer,
                  finer, finer, P(), P(), P(), P(), P()),
        out_specs=(P(("groups", "band", "mesh", "feat"), None), rows),
        check_vma=False,
    )
```

time: 208 us -> 53.6 us (0.26)
  waiting for transfers between devices: 106 us -> 0 us
  Pallas kernels: 0 us -> 37 us
  starting transfers between devices: 24.3 us -> 0 us
  local copies, waits for them, and re-layouts: 39.4 us -> 15.1 us
  other arithmetic: 14.4 us -> 0 us
  between operations: 14.7 us -> 0.75 us
  matrix products: 8.45 us -> 0 us
    all_to_all x3 -> x0, waiting for transfers between devices: 46.6 us -> none  [the longest x2 33.5 us: nearby_rows(): lax.all_to_all(buffer.reshape(3, columns, places, width), 'mesh', split_a...]
    pallas_call x0 -> x1, Pallas kernels: none -> 37 us  [per_device(): pl.pallas_call(functools.partial(kernel, nb, nm, cap_g, cap_h, cap_m), ou...]
    gather x9 -> x0, local copies, waits for them, and re-layouts: 34.5 us -> none  [the longest x3 11.6 us: sender_terms(): arrived = carry(jnp.take(source, send_list, axis=0))]
    psum x2 -> x0, waiting for transfers between devices: 34.1 us -> none  [per_device(): lax.psum(partial_terms.astype(jnp.bfloat16), 'feat').astype(jnp.float32)]
    ppermute x4 -> x0, waiting for transfers between devices: 25 us -> none  [shifted(): lax.ppermute(value, axis, [(source, source + steps) for source in range(l...]
    all_to_all x3 -> x0, starting transfers between devices: 13.9 us -> none  [the longest x2 8.15 us: nearby_rows(): lax.all_to_all(buffer.reshape(3, columns, places, width), 'mesh', split_a...]
    ppermute x4 -> x0, starting transfers between devices: 10.4 us -> none  [shifted(): lax.ppermute(value, axis, [(source, source + steps) for source in range(l...]
    dot_general x9 -> x0, matrix products: 8.45 us -> none  [the longest x2 4.33 us: aggregate(): jnp.dot(summed.astype(jnp.bfloat16), out_w, preferred_element_type=jnp.fl...]
  transfers between devices with their start and end apart: 9 -> 0, of which waited for: 9 -> 0; matrix products, arithmetic and copies ran while one was open for 5% -> 0% of each run, Pallas kernels for 0% -> 0%
where the time goes in v1:
time: 53.6 us; the launch traced here: 52.8 us
  Pallas kernels  37 us (69%)
  local copies, waits for them, and re-layouts  15.1 us (28%)
  between operations  0.75 us (1%)
    pallas_call x1, Pallas kernels, per_device(): pl.pallas_call(functools.partial(kernel, nb, nm, cap_g, cap_h, cap_m), ou...  37 us
    unnamed x42, local copies, waits for them, and re-layouts  11.2 us
    reshape x2, local copies, waits for them, and re-layouts, per_device(): row = lambda v: v.reshape(1, -1)  1.4 us

profile of v1, /device:TPU:0, one launch (start us, length us, event | category | flops | bytes accessed | tf_op | source)
XLA Modules:
  0.0 52.8 jit_solution(10906478525323913897)
XLA Ops:
  0.6 0.8 %reshape.49.g_send = s32[6,1,256]{2,1,0:T(1,128)S(1)} reshape(s32[1536]{0:T(1024)} %param.27) | data formatting | bytes 12288 | tf_op jit(solution)/shard_map/reshape | solution.py:289
  1.4 0.7 %reshape.50.g_slot = s32[1,1536]{1,0:T(1,128)S(1)} reshape(s32[1536]{0:T(1024)} %param.28) | data formatting | bytes 12288 | tf_op jit(solution)/shard_map/reshape | solution.py:286
  2.1 0.7 %reshape.51.g_recv = s32[1,1536]{1,0:T(1,128)S(1)} reshape(s32[1536]{0:T(1024)} %param.29) | data formatting | bytes 12288 | tf_op jit(solution)/shard_map/reshape | solution.py:286
  2.8 0.7 %reshape.59.m_send = s32[6,1,256]{2,1,0:T(1,128)S(1)} reshape(s32[1536]{0:T(1024)} %param.43) | data formatting | bytes 12288 | tf_op jit(solution)/shard_map/reshape | solution.py:293
  3.5 0.9 %reshape.60 = s32[512,3]{1,0:T(8,128)S(1)} reshape(s32[1536]{0:T(1024)} %param.44) | data formatting | bytes 12288 | tf_op jit(solution)/shard_map/reshape | solution.py:293
  4.4 0.0 copy-start.10
  4.4 0.0 copy-start.18
  4.4 0.0 copy-start.19
  4.5 0.1 copy.27
  4.6 0.0 copy-start.14
  4.6 0.0 copy-start.15
  4.6 0.0 copy-start.16
  4.6 0.0 copy-start.17
  4.7 0.6 %copy-done.10 = bf16[64,512]{1,0:T(8,128)(2,1)S(1)} copy-done((bf16[64,512]{1,0:T(8,128)(2,1)S(1)}, bf16[64,512]{1,0:T(8,128)(2,1)}, u32[]{:S(2)}) %copy-start.10) | copy-done | bytes 65560
  5.3 0.0 copy-done.12
  5.3 0.0 copy-done.13
  5.3 0.0 copy-done.14
  5.3 0.0 copy-done.15
  5.3 0.0 copy-done.16
  5.3 0.0 copy-done.17
  5.4 1.2 %copy-done = bf16[1024,512]{1,0:T(8,128)(2,1)S(1)} copy-done((bf16[1024,512]{1,0:T(8,128)(2,1)S(1)}, bf16[1024,512]{1,0:T(8,128)(2,1)}, u32[]{:S(2)}) %copy-start) | copy-done | bytes 1048600
  6.6 1.0 %copy-done.2 = bf16[512,512]{1,0:T(8,128)(2,1)S(1)} copy-done((bf16[512,512]{1,0:T(8,128)(2,1)S(1)}, bf16[512,512]{1,0:T(8,128)(2,1)}, u32[]{:S(2)}) %copy-start.2) | copy-done | bytes 524312
  7.6 1.0 %copy-done.3 = bf16[512,512]{1,0:T(8,128)(2,1)S(1)} copy-done((bf16[512,512]{1,0:T(8,128)(2,1)S(1)}, bf16[512,512]{1,0:T(8,128)(2,1)}, u32[]{:S(2)}) %copy-start.3) | copy-done | bytes 524312
  8.7 0.9 %copy-done.4 = bf16[512,256]{1,0:T(8,128)(2,1)S(1)} copy-done((bf16[512,256]{1,0:T(8,128)(2,1)S(1)}, bf16[512,256]{1,0:T(8,128)(2,1)}, u32[]{:S(2)}) %copy-start.4) | copy-done | bytes 262168
  9.6 0.9 %copy-done.5 = bf16[512,256]{1,0:T(8,128)(2,1)S(1)} copy-done((bf16[512,256]{1,0:T(8,128)(2,1)S(1)}, bf16[512,256]{1,0:T(8,128)(2,1)}, u32[]{:S(2)}) %copy-start.5) | copy-done | bytes 262168
  10.6 0.9 %copy-done.6 = bf16[256,512]{1,0:T(8,128)(2,1)S(1)} copy-done((bf16[256,512]{1,0:T(8,128)(2,1)S(1)}, bf16[256,512]{1,0:T(8,128)(2,1)}, u32[]{:S(2)}) %copy-start.6) | copy-done | bytes 262168
  11.5 0.9 %copy-done.7 = bf16[512,256]{1,0:T(8,128)(2,1)S(1)} copy-done((bf16[512,256]{1,0:T(8,128)(2,1)S(1)}, bf16[512,256]{1,0:T(8,128)(2,1)}, u32[]{:S(2)}) %copy-start.7) | copy-done | bytes 262168
  12.5 0.9 %copy-done.8 = bf16[512,256]{1,0:T(8,128)(2,1)S(1)} copy-done((bf16[512,256]{1,0:T(8,128)(2,1)S(1)}, bf16[512,256]{1,0:T(8,128)(2,1)}, u32[]{:S(2)}) %copy-start.8) | copy-done | bytes 262168
  13.4 0.9 %copy-done.9 = bf16[256,512]{1,0:T(8,128)(2,1)S(1)} copy-done((bf16[256,512]{1,0:T(8,128)(2,1)S(1)}, bf16[256,512]{1,0:T(8,128)(2,1)}, u32[]{:S(2)}) %copy-start.9) | copy-done | bytes 262168
  14.4 37.0 %shard_map.248 = (bf16[512,512]{1,0:T(8,128)(2,1)S(1)}, bf16[64,512]{1,0:T(8,128)(2,1)S(1)}) custom-call(bf16[1024,512]{1,0:T(8,128)(2,1)S(1)} %copy-done, bf16[64,512]{1,0:T(8,128)(2,1)S(1)} %copy-done.10, s32[6,1,256]{2,1,0:T(1,128)S(1)} %reshape.49.g_send, s32[1,1536]{1,0:T(1,128)S(1)} %reshape.50.g_slot, s32[1,1536]{1,0:T(1,128)S(1)} %reshape.51.g_recv, ...), custom_call_target="tpu_custom_call" | custom-call | tf_op jit(solution)/shard_map/pallas_call | solution.py:318
  51.4 0.8 %copy.30 = bf16[512,512]{1,0:T(8,128)(2,1)} copy(bf16[512,512]{1,0:T(8,128)(2,1)S(1)} %get-tuple-element.4) | data formatting | bytes 1048576
  52.2 0.6 %copy.31 = bf16[64,512]{1,0:T(8,128)(2,1)} copy(bf16[64,512]{1,0:T(8,128)(2,1)S(1)} %get-tuple-element.5) | data formatting | bytes 131072
  (18 shorter events, 0.0 us)
Async XLA Ops:
  0.6 4.0 %copy-start.1 = (bf16[512,512]{1,0:T(8,128)(2,1)S(1)}, bf16[512,512]{1,0:T(8,128)(2,1)}, u32[]{:S(2)}) copy-start(bf16[512,512]{1,0:T(8,128)(2,1)} %d_sw.1) | copy-start | bytes 1572868
  4.4 0.8 %copy-start.10 = (bf16[64,512]{1,0:T(8,128)(2,1)S(1)}, bf16[64,512]{1,0:T(8,128)(2,1)}, u32[]{:S(2)}) copy-start(bf16[64,512]{1,0:T(8,128)(2,1)} %mesh_ref.1) | copy-start | bytes 196612
  4.4 0.8 %copy-start.18 = (f32[256]{0:T(256)S(1)}, f32[256]{0:T(256)}, u32[]{:S(2)}) copy-start(f32[256]{0:T(256)} %param.32) | copy-start | bytes 3076
  4.4 0.8 %copy-start.19 = (f32[256]{0:T(256)S(1)}, f32[256]{0:T(256)}, u32[]{:S(2)}) copy-start(f32[256]{0:T(256)} %param.40) | copy-start | bytes 3076
  4.6 0.7 %copy-start.11 = (f32[512]{0:T(512)S(1)}, f32[512]{0:T(512)}, u32[]{:S(2)}) copy-start(f32[512]{0:T(512)} %param.34) | copy-start | bytes 6148
  4.6 0.7 %copy-start.12 = (s32[512]{0:T(512)S(1)}, s32[512]{0:T(512)}, u32[]{:S(2)}) copy-start(s32[512]{0:T(512)} %param.35) | copy-start | bytes 6148
  4.6 0.7 %copy-start.13 = (s32[512]{0:T(512)S(1)}, s32[512]{0:T(512)}, u32[]{:S(2)}) copy-start(s32[512]{0:T(512)} %param.36) | copy-start | bytes 6148
  4.6 0.7 %copy-start.14 = (s32[512]{0:T(512)S(1)}, s32[512]{0:T(512)}, u32[]{:S(2)}) copy-start(s32[512]{0:T(512)} %param.37) | copy-start | bytes 6148
  4.6 0.7 %copy-start.15 = (f32[512]{0:T(512)S(1)}, f32[512]{0:T(512)}, u32[]{:S(2)}) copy-start(f32[512]{0:T(512)} %param.42) | copy-start | bytes 6148
  4.6 0.7 %copy-start.16 = (f32[512]{0:T(512)S(1)}, f32[512]{0:T(512)}, u32[]{:S(2)}) copy-start(f32[512]{0:T(512)} %param.47) | copy-start | bytes 6148
  4.6 0.7 %copy-start.17 = (f32[512]{0:T(512)S(1)}, f32[512]{0:T(512)}, u32[]{:S(2)}) copy-start(f32[512]{0:T(512)} %param.49) | copy-start | bytes 6148
  5.4 1.2 %copy-start = (bf16[1024,512]{1,0:T(8,128)(2,1)S(1)}, bf16[1024,512]{1,0:T(8,128)(2,1)}, u32[]{:S(2)}) copy-start(bf16[1024,512]{1,0:T(8,128)(2,1)} %grid_ref.1) | copy-start | bytes 3145732
  6.6 1.0 %copy-start.2 = (bf16[512,512]{1,0:T(8,128)(2,1)S(1)}, bf16[512,512]{1,0:T(8,128)(2,1)}, u32[]{:S(2)}) copy-start(bf16[512,512]{1,0:T(8,128)(2,1)} %d_rw.1) | copy-start | bytes 1572868
  7.6 1.0 %copy-start.3 = (bf16[512,512]{1,0:T(8,128)(2,1)S(1)}, bf16[512,512]{1,0:T(8,128)(2,1)}, u32[]{:S(2)}) copy-start(bf16[512,512]{1,0:T(8,128)(2,1)} %d_ow.1) | copy-start | bytes 1572868
  8.7 0.9 %copy-start.4 = (bf16[512,256]{1,0:T(8,128)(2,1)S(1)}, bf16[512,256]{1,0:T(8,128)(2,1)}, u32[]{:S(2)}) copy-start(bf16[512,256]{1,0:T(8,128)(2,1)} %e_sw.1) | copy-start | bytes 786436
  9.6 0.9 %copy-start.5 = (bf16[512,256]{1,0:T(8,128)(2,1)S(1)}, bf16[512,256]{1,0:T(8,128)(2,1)}, u32[]{:S(2)}) copy-start(bf16[512,256]{1,0:T(8,128)(2,1)} %e_rw.1) | copy-start | bytes 786436
  10.6 0.9 %copy-start.6 = (bf16[256,512]{1,0:T(8,128)(2,1)S(1)}, bf16[256,512]{1,0:T(8,128)(2,1)}, u32[]{:S(2)}) copy-start(bf16[256,512]{1,0:T(8,128)(2,1)} %e_ow.1) | copy-start | bytes 786436
  11.5 0.9 %copy-start.7 = (bf16[512,256]{1,0:T(8,128)(2,1)S(1)}, bf16[512,256]{1,0:T(8,128)(2,1)}, u32[]{:S(2)}) copy-start(bf16[512,256]{1,0:T(8,128)(2,1)} %p_sw.1) | copy-start | bytes 786436
  12.5 0.9 %copy-start.8 = (bf16[512,256]{1,0:T(8,128)(2,1)S(1)}, bf16[512,256]{1,0:T(8,128)(2,1)}, u32[]{:S(2)}) copy-start(bf16[512,256]{1,0:T(8,128)(2,1)} %p_rw.1) | copy-start | bytes 786436
  13.4 0.9 %copy-start.9 = (bf16[256,512]{1,0:T(8,128)(2,1)S(1)}, bf16[256,512]{1,0:T(8,128)(2,1)}, u32[]{:S(2)}) copy-start(bf16[256,512]{1,0:T(8,128)(2,1)} %p_ow.1) | copy-start | bytes 786436

commit v2 on v1

--- a/solution.py
+++ b/solution.py
@@ -44,19 +44,48 @@
     return parts[0] if len(parts) == 1 else jnp.concatenate(parts, axis=1)
 
 
-def kernel(
-    nb, nm, cap_g, cap_h, cap_m,
-    grid_ref, mesh_ref, g_send, g_slot, g_recv, e_sw, e_rw, e_b, e_ow, e_g,
-    p_send, p_slot, p_recv, p_sw, p_rw, p_b, p_ow, p_g,
-    m_send, m_slot, d_sw, d_rw, d_b, d_ow, d_g,
-    grid_out, mesh_out,
-    gp, ebuf, erecv, ecol, hid, hid2, own_term, pbuf, precv, iref, dcol, dproj, dtab,
-    part, other,
-    es, er, is_, ir, ps, pr, ds, dr, fs, fr,
-):
-    shards = nb * nm
+NAMES = (
+    "grid", "mesh", "g_send", "g_slot", "g_recv", "e_sw", "e_rw", "e_b", "e_ow", "e_g",
+    "p_send", "p_slot", "p_recv", "p_sw", "p_rw", "p_b", "p_ow", "p_g",
+    "m_send", "m_slot", "d_sw", "d_rw", "d_b", "d_ow", "d_g",
+)
+FIRST = ("g_send", "e_sw", "grid", "m_send")
+SECOND = ("d_rw", "d_b", "mesh", "e_rw", "e_b", "m_slot", "g_slot", "g_recv", "e_ow", "e_g")
+THIRD = ("p_send", "p_slot", "p_recv", "p_sw", "p_rw", "p_b", "p_ow", "p_g", "d_sw", "d_ow", "d_g")
+
+
+def kernel(nb, nm, cap_g, cap_h, cap_m, *refs):
+    count = len(NAMES)
+    sources = dict(zip(NAMES, refs[:count]))
+    grid_out, mesh_out = refs[count : count + 2]
+    here = dict(zip(NAMES, refs[count + 2 : 2 * count + 2]))
+    (
+        gp, ebuf, erecv, ecol, hid, hid2, gcol, own_term, pbuf, precv, mbuf, iref, dcol, dproj, dtab,
+        part, other, ls,
+        es, er, is_, ir, ps, pr, ds, dr, fs, fr,
+    ) = refs[2 * count + 2 :]
+
+    def fetch(name):
+        return pltpu.make_async_copy(sources[name], here[name], ls.at[NAMES.index(name)])
+
+    def ready(*names):
+        for name in names:
+            fetch(name).wait()
+
+    for name in FIRST:
+        fetch(name).start()
+
+    def flat(name):
+        value = here[name][...]
+        return value.reshape(1, value.shape[0])
+
+    grid_ref, mesh_ref = here["grid"], here["mesh"]
+    e_sw, e_rw, e_ow = here["e_sw"], here["e_rw"], here["e_ow"]
+    p_sw, p_rw, p_ow = here["p_sw"], here["p_rw"], here["p_ow"]
+    d_sw, d_rw, d_ow = here["d_sw"], here["d_rw"], here["d_ow"]
     band, col, feat = lax.axis_index("band"), lax.axis_index("mesh"), lax.axis_index("feat")
     me = band * nm + col
+    shards = nb * nm
     mrows = mesh_ref.shape[0]
     half = grid_out.shape[0]
     dh = e_sw.shape[1]
@@ -71,6 +100,9 @@
         pl.semaphore_signal(barrier, inc=1, device_id=at_shard(peer), device_id_type=MESH)
     pl.semaphore_signal(barrier, inc=1, device_id={"feat": 1 - feat}, device_id_type=MESH)
 
+    for name in SECOND:
+        fetch(name).start()
+    ready("g_send", "e_sw", "grid", "m_send")
     gp[...] = dot(grid_ref[...], e_sw[...]).astype(BF)
     for d, edge in ((0, 0), (2, nb - 1)):
         @pl.when(band == edge)
@@ -119,12 +151,20 @@
 
     order = [(d, o) for d in (0, 2, 1) for o in reversed(range(nm)) if (d, o) != (1, 0)]
 
-    for d, o in order:
-        when(to_there(d), lambda d=d, o=o: near_copy(lambda i: m_send.at[i], iref, is_, ir, d, o).start())
-    iref[nm + col] = m_send[nm + col]
+    for name in THIRD:
+        fetch(name).start()
+
+    for i in range(near):
+        mbuf[i] = flat("m_send")[:, i * cap_m : (i + 1) * cap_m]
+    for d, o in order:
+        when(to_there(d), lambda d=d, o=o: near_copy(lambda i: mbuf.at[i], iref, is_, ir, d, o).start())
+    iref[nm + col] = mbuf[nm + col]
+
+    for i in range(near):
+        gcol[i] = columns(flat("g_send")[:, i * cap_g : (i + 1) * cap_g])
 
     def gathered(i):
-        return dot(pick(columns(g_send[i]), gp.shape[0]), gp[...]).astype(BF)
+        return dot(pick(gcol[i], gp.shape[0]), gp[...]).astype(BF)
 
     for d, o in order:
         def send(d=d, o=o):
@@ -134,11 +174,12 @@
         when(to_there(d), send)
     erecv[nm + col] = gathered(nm + col)
 
+    ready(*SECOND)
     own = pl.ds(pl.multiple_of(feat * half, half), half)
-    own_term[...] = dot(grid_ref[own, :], d_rw[...]) + d_b[...]
+    own_term[...] = dot(grid_ref[own, :], d_rw[...]) + flat("d_b")
 
     def split_term(values, weight, bias):
-        term = dot(values, weight[...]) + bias[...]
+        term = dot(values, weight[...]) + bias
         high = term.astype(BF)
         return jnp.concatenate([high, (term - high.astype(F32)).astype(BF)], axis=0)
 
@@ -150,14 +191,13 @@
         single = pick(cols, mrows)
         return jnp.concatenate([single, single], axis=1)
 
-    eterm = split_term(mesh_ref[...], e_rw, e_b)
+    eterm = split_term(mesh_ref[...], e_rw, flat("e_b"))
 
     for d, o in order:
         when(from_there(d), lambda d=d, o=o: near_arrival(iref, is_, ir, d, o).wait_recv())
-    nedge = m_slot.shape[0] * m_slot.shape[2]
     tables = [columns(iref[i]).astype(F32).astype(BF) for i in range(near)]
     for k in range(3):
-        slots = columns(m_slot[k])
+        slots = columns(flat("m_slot")[:, k * half : (k + 1) * half])
         block = jnp.zeros(slots.shape, jnp.int32)
         row = jnp.zeros(slots.shape, F32)
         for i in range(near):
@@ -166,8 +206,8 @@
                 block = block + jnp.where(slots >= i * cap_m, mrows, 0)
         dcol[pl.ds(k * half, half), :] = block + (row + 0.5).astype(jnp.int32)
 
-    ecol[0] = columns(g_slot[...])
-    ecol[1] = columns(g_recv[...])
+    ecol[0] = columns(flat("g_slot"))
+    ecol[1] = columns(flat("g_recv"))
     for d, o in order:
         when(from_there(d), lambda d=d, o=o: near_arrival(erecv, es, er, d, o).wait_recv())
     chunk = 256
@@ -183,7 +223,7 @@
 
     def finish(base, recv, hidden, ow, gain, n):
         place = lax.broadcasted_iota(jnp.int32, (mrows, recv.shape[1]), 0)
-        onto = jnp.where(recv[...] == place, 1.0, 0.0).astype(BF)
+        onto = jnp.where(recv == place, 1.0, 0.0).astype(BF)
         summed = dot(onto, hidden[...]).astype(BF)
         part[n] = dot(summed, ow[...]).astype(BF)
         copy = pltpu.make_async_remote_copy(
@@ -193,12 +233,13 @@
         copy.start()
         copy.wait()
         total = part[n].astype(F32) + other[n].astype(F32)
-        return (base.astype(F32) + normed(total, gain[...])).astype(BF)
-
-    psend_pick = pick(columns(p_send[...]), mrows)
-    pslot_pick = pick(columns(p_slot[...]), shards * cap_h)
-    precv_pick = pick2(columns(p_recv[...]))
-    first = finish(mesh_ref[...], g_recv, hid, e_ow, e_g, 0)
+        return (base.astype(F32) + normed(total, gain)).astype(BF)
+
+    ready(*THIRD)
+    psend_pick = pick(columns(flat("p_send")), mrows)
+    pslot_pick = pick(columns(flat("p_slot")), shards * cap_h)
+    precv_pick = pick2(columns(flat("p_recv")))
+    first = finish(mesh_ref[...], flat("g_recv"), hid, e_ow, flat("e_g"), 0)
 
     mproj = dot(first, p_sw[...]).astype(BF)
     pbuf[...] = dot(psend_pick, mproj).astype(BF).reshape(pbuf.shape)
@@ -220,12 +261,12 @@
     for o in range(1, shards):
         proc_copy(o).start()
     precv[me] = pbuf[me]
-    pterm = dot(precv_pick, split_term(first, p_rw, p_b))
+    pterm = dot(precv_pick, split_term(first, p_rw, flat("p_b")))
     for o in range(1, shards):
         proc_arrival(o).wait_recv()
     pre = dot(pslot_pick, precv[...].reshape(shards * cap_h, dh)) + pterm
     hid2[...] = silu(pre).astype(BF)
-    last = finish(first, p_recv, hid2, p_ow, p_g, 1)
+    last = finish(first, flat("p_recv"), hid2, p_ow, flat("p_g"), 1)
     mesh_out[...] = last
 
     projected = dot(last, d_sw[...]).astype(BF)
@@ -243,19 +284,19 @@
         table = dtab[...].reshape(near * mrows, dtab.shape[2])
         summed = jnp.zeros(term.shape, F32)
         for k in range(3):
-            idx = dcol[pl.ds(pl.multiple_of(k * half + c * dchunk, dchunk), dchunk), :]
+            idx = dcol[pl.ds(3 * c * dchunk + k, dchunk, stride=3), :]
             pre = dot(pick(idx, near * mrows), table) + term
             summed = summed + silu(pre).astype(BF).astype(F32)
         decoded = dot(summed.astype(BF), d_ow[...])
         base = grid_ref[pl.ds(pl.multiple_of(feat * half + c * dchunk, dchunk), dchunk), :]
-        grid_out[rows, :] = (base.astype(F32) + normed(decoded, d_g[...])).astype(BF)
+        grid_out[rows, :] = (base.astype(F32) + normed(decoded, flat("d_g"))).astype(BF)
         return carry
 
     lax.fori_loop(0, half // dchunk, decode, 0)
 
     for d, o in order:
         def done(d=d, o=o):
-            near_copy(lambda i: m_send.at[i], iref, is_, ir, d, o).wait_send()
+            near_copy(lambda i: mbuf.at[i], iref, is_, ir, d, o).wait_send()
             near_copy(lambda i: ebuf.at[i], erecv, es, er, d, o).wait_send()
             near_copy(lambda i: dproj, dtab, ds, dr, d, o).wait_send()
         when(to_there(d), done)
@@ -280,37 +321,38 @@
     cap_h = proc_send.shape[0] // shards
     if cap_h % 16:
         padded = -(-cap_h // 16) * 16
-        proc_send = jnp.pad(proc_send.reshape(shards, cap_h), ((0, 0), (0, padded - cap_h)))
+        proc_send = jnp.pad(proc_send.reshape(shards, cap_h), ((0, 0), (0, padded - cap_h))).reshape(-1)
         proc_slot = proc_slot // cap_h * padded + proc_slot % cap_h
         cap_h = padded
-    row = lambda v: v.reshape(1, -1)
     args = (
         grid_latent, mesh_latent,
-        g2m_send.reshape(near, 1, cap_g), row(g2m_slot), row(g2m_recv),
-        enc_send_w, enc_recv_w, row(enc_bias), enc_out_w, row(enc_gain),
-        row(proc_send), row(proc_slot), row(proc_recv),
-        proc_send_w, proc_recv_w, row(proc_bias), proc_out_w, row(proc_gain),
-        m2g_send.reshape(near, 1, cap_m), m2g_slot.reshape(half, 3).T.reshape(3, 1, half),
-        dec_send_w, dec_recv_w, row(dec_bias), dec_out_w, row(dec_gain),
+        g2m_send, g2m_slot, g2m_recv, enc_send_w, enc_recv_w, enc_bias, enc_out_w, enc_gain,
+        proc_send, proc_slot, proc_recv,
+        proc_send_w, proc_recv_w, proc_bias, proc_out_w, proc_gain,
+        m2g_send, m2g_slot, dec_send_w, dec_recv_w, dec_bias, dec_out_w, dec_gain,
     )
+    hbm = pl.BlockSpec(memory_space=pltpu.HBM)
     vmem = pl.BlockSpec(memory_space=pltpu.VMEM)
     dma = pltpu.SemaphoreType.DMA
-    scratch = [
+    scratch = [pltpu.VMEM(v.shape, v.dtype) for v in args] + [
         pltpu.VMEM((rows, dh), BF),
         pltpu.VMEM((near, cap_g, dh), BF),
         pltpu.VMEM((near, cap_g, dh), BF),
         pltpu.VMEM((2, g2m_slot.shape[0], LANES), jnp.int32),
         pltpu.VMEM((g2m_slot.shape[0], dh), BF),
         pltpu.VMEM((proc_slot.shape[0], dh), BF),
+        pltpu.VMEM((near, cap_g, LANES), jnp.int32),
         pltpu.VMEM((half, width), F32),
         pltpu.VMEM((shards, cap_h, dh), BF),
         pltpu.VMEM((shards, cap_h, dh), BF),
+        pltpu.VMEM((near, 1, cap_m), jnp.int32),
         pltpu.VMEM((near, 1, cap_m), jnp.int32),
         pltpu.VMEM((3 * half, LANES), jnp.int32),
         pltpu.VMEM((mrows, width), BF),
         pltpu.VMEM((near, mrows, width), BF),
         pltpu.VMEM((2, mrows, width), BF),
         pltpu.VMEM((2, mrows, width), BF),
+        dma((len(args),)),
         dma((near,)), dma((near,)), dma((near,)), dma((near,)),
         dma((shards,)), dma((shards,)), dma((near,)), dma((near,)),
         dma((2,)), dma((2,)),
@@ -321,11 +363,11 @@
             jax.ShapeDtypeStruct((half, width), BF),
             jax.ShapeDtypeStruct((mrows, width), BF),
         ),
-        in_specs=[vmem] * len(args),
+        in_specs=[hbm] * len(args),
         out_specs=(vmem, vmem),
         scratch_shapes=scratch,
         compiler_params=pltpu.CompilerParams(
-            collective_id=0, has_side_effects=True, vmem_limit_bytes=48 * 1024 * 1024
+            collective_id=0, has_side_effects=True, vmem_limit_bytes=64 * 1024 * 1024
         ),
     )(*args)
     return (grid_out, mesh_out)

time: 53.6 us -> 41.9 us (0.78); the launches traced: 52.8 us -> 41.7 us
  local copies, waits for them, and re-layouts: 15.1 us -> 2.53 us
  Pallas kernels: 37 us -> 38.5 us
    unnamed x42 -> x4, local copies, waits for them, and re-layouts: 11.2 us -> 2.53 us
    reshape x7 -> x0, local copies, waits for them, and re-layouts: 3.89 us -> none  [the longest x2 1.4 us: per_device(): row = lambda v: v.reshape(1, -1)]
    pallas_call x1, Pallas kernels: 37 us -> 38.5 us  [per_device(): pl.pallas_call(functools.partial(kernel, nb, nm, cap_g, cap_h, cap_m), ou...]
where the time goes in v2:
time: 41.9 us; the launch traced here: 41.7 us
  Pallas kernels  38.5 us (92%)
  local copies, waits for them, and re-layouts  2.53 us (6%)
  between operations  0.66 us (2%)
    pallas_call x1, Pallas kernels, per_device(): pl.pallas_call(functools.partial(kernel, nb, nm, cap_g, cap_h, cap_m), ou...  38.5 us
    unnamed x4, local copies, waits for them, and re-layouts  2.53 us

profile of v2, /device:TPU:0, one launch (start us, length us, event | category | flops | bytes accessed | tf_op | source)
XLA Modules:
  0.0 41.7 jit_solution(1534237241412423184)
XLA Ops:
  0.6 38.5 %shard_map.248 = (bf16[512,512]{1,0:T(8,128)(2,1)}, bf16[64,512]{1,0:T(8,128)(2,1)}) custom-call(bf16[1024,512]{1,0:T(8,128)(2,1)} %refs_0_.1, bf16[64,512]{1,0:T(8,128)(2,1)} %refs_1_.1, s32[1536]{0:T(1024)} %refs_2_.1, s32[1536]{0:T(1024)} %refs_3_.1, s32[1536]{0:T(1024)} %refs_4_.1, bf16[512,256]{1,0:T(8,128)(2,1)} %refs_5_.1, bf16[512,256]{1,0:T(8,128)(2,1)} %refs_6_.1, ...), custom_call_target="tpu_custom_call" | custom-call | tf_op jit(solution)/shard_map/pallas_call | solution.py:360
  39.1 0.0 copy-start
  39.1 1.9 %copy.29 = bf16[512,512]{1,0:T(8,128)(2,1)} copy(bf16[512,512]{1,0:T(8,128)(2,1)} %get-tuple-element.4) | data formatting | bytes 1048576
  41.0 0.0 copy-done
  41.0 0.6 %copy.30 = bf16[64,512]{1,0:T(8,128)(2,1)} copy(bf16[64,512]{1,0:T(8,128)(2,1)S(1)} %copy-done) | data formatting | bytes 131072
Async XLA Ops:
  39.1 1.9 %copy-start = (bf16[64,512]{1,0:T(8,128)(2,1)S(1)}, bf16[64,512]{1,0:T(8,128)(2,1)}, u32[]{:S(2)}) copy-start(bf16[64,512]{1,0:T(8,128)(2,1)} %get-tuple-element.5) | copy-start | bytes 196612

commit v3 on v2

--- a/solution.py
+++ b/solution.py
@@ -60,9 +60,9 @@
     grid_out, mesh_out = refs[count : count + 2]
     here = dict(zip(NAMES, refs[count + 2 : 2 * count + 2]))
     (
-        gp, ebuf, erecv, ecol, hid, hid2, gcol, own_term, pbuf, precv, mbuf, iref, dcol, dproj, dtab,
+        gp, ebuf, erecv, ecol, hid, acc, hid2, gcol, own_term, pbuf, precv, mbuf, iref, dcol, dproj, dtab,
         part, other, ls,
-        es, er, is_, ir, ps, pr, ds, dr, fs, fr,
+        es, er, is_, ir, ps, pr, ds, dr, fs, fr, ws, wr,
     ) = refs[2 * count + 2 :]
 
     def fetch(name):
@@ -111,7 +111,8 @@
                 i = d * nm + j
                 erecv[i] = jnp.zeros(erecv.shape[1:], BF)
                 iref[i] = jnp.zeros(iref.shape[1:], jnp.int32)
-                dtab[i] = jnp.zeros(dtab.shape[1:], BF)
+                for f in range(2):
+                    dtab[f, i] = jnp.zeros(dtab.shape[2:], BF)
 
     pl.semaphore_wait(barrier, shards)
 
@@ -149,7 +150,9 @@
         else:
             pl.when(cond)(f)
 
-    order = [(d, o) for d in (0, 2, 1) for o in reversed(range(nm)) if (d, o) != (1, 0)]
+    across = [(d, o) for d in (0, 2, 1) for o in range(1, nm)]
+    along = [(0, 0), (2, 0)]
+    order = across + along
 
     for name in THIRD:
         fetch(name).start()
@@ -208,18 +211,38 @@
 
     ecol[0] = columns(flat("g_slot"))
     ecol[1] = columns(flat("g_recv"))
-    for d, o in order:
-        when(from_there(d), lambda d=d, o=o: near_arrival(erecv, es, er, d, o).wait_recv())
     chunk = 256
 
-    def edges(c, carry):
-        rows = pl.ds(pl.multiple_of(c * chunk, chunk), chunk)
-        pre = dot(pick(ecol[0, rows, :], near * cap_g), erecv[...].reshape(near * cap_g, dh))
-        pre = pre.astype(BF).astype(F32) + dot(pick2(ecol[1, rows, :]), eterm)
-        hid[rows, :] = silu(pre).astype(BF)
-        return carry
-
-    lax.fori_loop(0, hid.shape[0] // chunk, edges, 0)
+    def block_terms(rows, blocks):
+        cols = ecol[0, rows, :]
+        hot = jnp.concatenate([pick(cols - i * cap_g, cap_g) for i in blocks], axis=1)
+        return dot(hot, jnp.concatenate([erecv[i] for i in blocks], axis=0))
+
+    def chunks(body):
+        def step(c, carry):
+            body(pl.ds(pl.multiple_of(c * chunk, chunk), chunk))
+            return carry
+
+        lax.fori_loop(0, hid.shape[0] // chunk, step, 0)
+
+    def arrived(pairs):
+        for d, o in pairs:
+            when(from_there(d), lambda d=d, o=o: near_arrival(erecv, es, er, d, o).wait_recv())
+
+    arrived(along)
+
+    def early(rows):
+        acc[rows, :] = block_terms(rows, [d * nm + col for d in range(3)]) + dot(
+            pick2(ecol[1, rows, :]), eterm
+        )
+
+    def late(rows):
+        blocks = [d * nm + lax.rem(col + o, nm) for d in range(3) for o in range(1, nm)]
+        hid[rows, :] = silu(acc[rows, :] + block_terms(rows, blocks)).astype(BF)
+
+    chunks(early)
+    arrived(across)
+    chunks(late)
 
     def finish(base, recv, hidden, ow, gain, n):
         place = lax.broadcasted_iota(jnp.int32, (mrows, recv.shape[1]), 0)
@@ -269,23 +292,43 @@
     last = finish(first, flat("p_recv"), hid2, p_ow, flat("p_g"), 1)
     mesh_out[...] = last
 
-    projected = dot(last, d_sw[...]).astype(BF)
+    side = dproj.shape[1]
+    projected = dot(last, d_sw[:, pl.ds(pl.multiple_of(feat * side, side), side)]).astype(BF)
     dproj[...] = projected
     for d, o in order:
-        when(to_there(d), lambda d=d, o=o: near_copy(lambda i: dproj, dtab, ds, dr, d, o).start())
-    dtab[nm + col] = projected
-    for d, o in order:
-        when(from_there(d), lambda d=d, o=o: near_arrival(dtab, ds, dr, d, o).wait_recv())
+        when(to_there(d), lambda d=d, o=o: near_copy(lambda i: dproj, dtab.at[feat], ds, dr, d, o).start())
+    dtab[feat, nm + col] = projected
+
+    def passed(i, half_of):
+        return pltpu.make_async_remote_copy(
+            src_ref=dtab.at[half_of, i], dst_ref=dtab.at[half_of, i],
+            send_sem=ws.at[i], recv_sem=wr.at[i],
+            device_id={"feat": 1 - feat}, device_id_type=MESH,
+        )
+
+    passed(nm + col, feat).start()
+    hops = along + [(1, o) for o in range(1, nm)] + [p for p in across if p[0] != 1]
+
+    def pass_on(d, o):
+        near_arrival(dtab.at[feat], ds, dr, d, o).wait_recv()
+        passed(d * nm + lax.rem(col + o, nm), feat).start()
+
+    for d, o in hops:
+        when(from_there(d), lambda d=d, o=o: pass_on(d, o))
+    for d, o in [(1, 0)] + hops:
+        when(from_there(d), lambda d=d, o=o: passed(
+            d * nm + lax.rem(col + o, nm), 1 - feat).wait_recv())
     dchunk = 128
 
     def decode(c, carry):
         rows = pl.ds(pl.multiple_of(c * dchunk, dchunk), dchunk)
         term = own_term[rows, :]
-        table = dtab[...].reshape(near * mrows, dtab.shape[2])
+        tables = [dtab[f].reshape(near * mrows, side) for f in range(2)]
         summed = jnp.zeros(term.shape, F32)
         for k in range(3):
             idx = dcol[pl.ds(3 * c * dchunk + k, dchunk, stride=3), :]
-            pre = dot(pick(idx, near * mrows), table) + term
+            hot = pick(idx, near * mrows)
+            pre = jnp.concatenate([dot(hot, t) for t in tables], axis=1) + term
             summed = summed + silu(pre).astype(BF).astype(F32)
         decoded = dot(summed.astype(BF), d_ow[...])
         base = grid_ref[pl.ds(pl.multiple_of(feat * half + c * dchunk, dchunk), dchunk), :]
@@ -298,8 +341,11 @@
         def done(d=d, o=o):
             near_copy(lambda i: mbuf.at[i], iref, is_, ir, d, o).wait_send()
             near_copy(lambda i: ebuf.at[i], erecv, es, er, d, o).wait_send()
-            near_copy(lambda i: dproj, dtab, ds, dr, d, o).wait_send()
+            near_copy(lambda i: dproj, dtab.at[feat], ds, dr, d, o).wait_send()
         when(to_there(d), done)
+    for d, o in [(1, 0)] + hops:
+        when(from_there(d), lambda d=d, o=o: passed(
+            d * nm + lax.rem(col + o, nm), feat).wait_send())
     for o in range(1, shards):
         proc_copy(o).wait_send()
 
@@ -340,6 +386,7 @@
         pltpu.VMEM((near, cap_g, dh), BF),
         pltpu.VMEM((2, g2m_slot.shape[0], LANES), jnp.int32),
         pltpu.VMEM((g2m_slot.shape[0], dh), BF),
+        pltpu.VMEM((g2m_slot.shape[0], dh), F32),
         pltpu.VMEM((proc_slot.shape[0], dh), BF),
         pltpu.VMEM((near, cap_g, LANES), jnp.int32),
         pltpu.VMEM((half, width), F32),
@@ -348,14 +395,14 @@
         pltpu.VMEM((near, 1, cap_m), jnp.int32),
         pltpu.VMEM((near, 1, cap_m), jnp.int32),
         pltpu.VMEM((3 * half, LANES), jnp.int32),
-        pltpu.VMEM((mrows, width), BF),
-        pltpu.VMEM((near, mrows, width), BF),
+        pltpu.VMEM((mrows, width // 2), BF),
+        pltpu.VMEM((2, near, mrows, width // 2), BF),
         pltpu.VMEM((2, mrows, width), BF),
         pltpu.VMEM((2, mrows, width), BF),
         dma((len(args),)),
         dma((near,)), dma((near,)), dma((near,)), dma((near,)),
         dma((shards,)), dma((shards,)), dma((near,)), dma((near,)),
-        dma((2,)), dma((2,)),
+        dma((2,)), dma((2,)), dma((near,)), dma((near,)),
     ]
     grid_out, mesh_out = pl.pallas_call(
         functools.partial(kernel, nb, nm, cap_g, cap_h, cap_m),

time: 41.9 us -> 42 us (level); the launches traced: 41.7 us -> 41.1 us
  Pallas kernels: 38.5 us -> 38 us
    pallas_call x1, Pallas kernels: 38.5 us -> 38 us  [per_device(): pl.pallas_call(functools.partial(kernel, nb, nm, cap_g, cap_h, cap_m), ou...]
where the time goes in v3:
time: 42 us; the launch traced here: 41.1 us
  Pallas kernels  38 us (90%)
  local copies, waits for them, and re-layouts  2.53 us (6%)
  between operations  0.66 us (2%)
    pallas_call x1, Pallas kernels, per_device(): pl.pallas_call(functools.partial(kernel, nb, nm, cap_g, cap_h, cap_m), ou...  38 us
    unnamed x4, local copies, waits for them, and re-layouts  2.53 us

profile of v3, /device:TPU:0, one launch (start us, length us, event | category | flops | bytes accessed | tf_op | source)
XLA Modules:
  0.0 41.1 jit_solution(17377214261036218281)
XLA Ops:
  0.6 38.0 %shard_map.248 = (bf16[512,512]{1,0:T(8,128)(2,1)}, bf16[64,512]{1,0:T(8,128)(2,1)}) custom-call(bf16[1024,512]{1,0:T(8,128)(2,1)} %refs_0_.1, bf16[64,512]{1,0:T(8,128)(2,1)} %refs_1_.1, s32[1536]{0:T(1024)} %refs_2_.1, s32[1536]{0:T(1024)} %refs_3_.1, s32[1536]{0:T(1024)} %refs_4_.1, bf16[512,256]{1,0:T(8,128)(2,1)} %refs_5_.1, bf16[512,256]{1,0:T(8,128)(2,1)} %refs_6_.1, ...), custom_call_target="tpu_custom_call" | custom-call | tf_op jit(solution)/shard_map/pallas_call | solution.py:407
  38.6 0.0 copy-start
  38.6 1.9 %copy.29 = bf16[512,512]{1,0:T(8,128)(2,1)} copy(bf16[512,512]{1,0:T(8,128)(2,1)} %get-tuple-element.4) | data formatting | bytes 1048576
  40.5 0.0 copy-done
  40.5 0.6 %copy.30 = bf16[64,512]{1,0:T(8,128)(2,1)} copy(bf16[64,512]{1,0:T(8,128)(2,1)S(1)} %copy-done) | data formatting | bytes 131072
Async XLA Ops:
  38.6 1.9 %copy-start = (bf16[64,512]{1,0:T(8,128)(2,1)S(1)}, bf16[64,512]{1,0:T(8,128)(2,1)}, u32[]{:S(2)}) copy-start(bf16[64,512]{1,0:T(8,128)(2,1)} %get-tuple-element.5) | copy-start | bytes 196612

commit v4 on v2

--- a/solution.py
+++ b/solution.py
@@ -149,7 +149,7 @@
         else:
             pl.when(cond)(f)
 
-    order = [(d, o) for d in (0, 2, 1) for o in reversed(range(nm)) if (d, o) != (1, 0)]
+    order = [(d, o) for d in (0, 2, 1) for o in range(1, nm)] + [(0, 0), (2, 0)]
 
     for name in THIRD:
         fetch(name).start()
@@ -210,7 +210,7 @@
     ecol[1] = columns(flat("g_recv"))
     for d, o in order:
         when(from_there(d), lambda d=d, o=o: near_arrival(erecv, es, er, d, o).wait_recv())
-    chunk = 256
+    chunk = 768
 
     def edges(c, carry):
         rows = pl.ds(pl.multiple_of(c * chunk, chunk), chunk)
@@ -276,7 +276,7 @@
     dtab[nm + col] = projected
     for d, o in order:
         when(from_there(d), lambda d=d, o=o: near_arrival(dtab, ds, dr, d, o).wait_recv())
-    dchunk = 128
+    dchunk = 512
 
     def decode(c, carry):
         rows = pl.ds(pl.multiple_of(c * dchunk, dchunk), dchunk)

time: 41.9 us -> 39.5 us (0.943)
  Pallas kernels: 38.5 us -> 36.2 us
    pallas_call x1, Pallas kernels: 38.5 us -> 36.2 us  [per_device(): pl.pallas_call(functools.partial(kernel, nb, nm, cap_g, cap_h, cap_m), ou...]
where the time goes in v4:
time: 39.5 us; the launch traced here: 39.3 us
  Pallas kernels  36.2 us (92%)
  local copies, waits for them, and re-layouts  2.53 us (6%)
  between operations  0.66 us (2%)
    pallas_call x1, Pallas kernels, per_device(): pl.pallas_call(functools.partial(kernel, nb, nm, cap_g, cap_h, cap_m), ou...  36.2 us
    unnamed x4, local copies, waits for them, and re-layouts  2.53 us

profile of v4, /device:TPU:0, one launch (start us, length us, event | category | flops | bytes accessed | tf_op | source)
XLA Modules:
  0.0 39.3 jit_solution(17343947605574345010)
XLA Ops:
  0.6 36.2 %shard_map.248 = (bf16[512,512]{1,0:T(8,128)(2,1)}, bf16[64,512]{1,0:T(8,128)(2,1)}) custom-call(bf16[1024,512]{1,0:T(8,128)(2,1)} %refs_0_.1, bf16[64,512]{1,0:T(8,128)(2,1)} %refs_1_.1, s32[1536]{0:T(1024)} %refs_2_.1, s32[1536]{0:T(1024)} %refs_3_.1, s32[1536]{0:T(1024)} %refs_4_.1, bf16[512,256]{1,0:T(8,128)(2,1)} %refs_5_.1, bf16[512,256]{1,0:T(8,128)(2,1)} %refs_6_.1, ...), custom_call_target="tpu_custom_call" | custom-call | tf_op jit(solution)/shard_map/pallas_call | solution.py:360
  36.8 0.0 copy-start
  36.8 1.9 %copy.29 = bf16[512,512]{1,0:T(8,128)(2,1)} copy(bf16[512,512]{1,0:T(8,128)(2,1)} %get-tuple-element.4) | data formatting | bytes 1048576
  38.7 0.0 copy-done
  38.7 0.6 %copy.30 = bf16[64,512]{1,0:T(8,128)(2,1)} copy(bf16[64,512]{1,0:T(8,128)(2,1)S(1)} %copy-done) | data formatting | bytes 131072
Async XLA Ops:
  36.8 1.9 %copy-start = (bf16[64,512]{1,0:T(8,128)(2,1)S(1)}, bf16[64,512]{1,0:T(8,128)(2,1)}, u32[]{:S(2)}) copy-start(bf16[64,512]{1,0:T(8,128)(2,1)} %get-tuple-element.5) | copy-start | bytes 196612

commit v5 on v4

--- a/solution.py
+++ b/solution.py
@@ -208,6 +208,15 @@
 
     ecol[0] = columns(flat("g_slot"))
     ecol[1] = columns(flat("g_recv"))
+    ready(*THIRD)
+    psend_pick = pick(columns(flat("p_send")), mrows)
+    pslot_pick = pick(columns(flat("p_slot")), shards * cap_h)
+    precv_pick = pick2(columns(flat("p_recv")))
+    def onto(recv):
+        place = lax.broadcasted_iota(jnp.int32, (mrows, recv.shape[1]), 0)
+        return jnp.where(recv == place, 1.0, 0.0).astype(BF)
+
+    g_onto, p_onto = onto(flat("g_recv")), onto(flat("p_recv"))
     for d, o in order:
         when(from_there(d), lambda d=d, o=o: near_arrival(erecv, es, er, d, o).wait_recv())
     chunk = 768
@@ -222,9 +231,7 @@
     lax.fori_loop(0, hid.shape[0] // chunk, edges, 0)
 
     def finish(base, recv, hidden, ow, gain, n):
-        place = lax.broadcasted_iota(jnp.int32, (mrows, recv.shape[1]), 0)
-        onto = jnp.where(recv == place, 1.0, 0.0).astype(BF)
-        summed = dot(onto, hidden[...]).astype(BF)
+        summed = dot(recv, hidden[...]).astype(BF)
         part[n] = dot(summed, ow[...]).astype(BF)
         copy = pltpu.make_async_remote_copy(
             src_ref=part.at[n], dst_ref=other.at[n], send_sem=fs.at[n], recv_sem=fr.at[n],
@@ -235,11 +242,7 @@
         total = part[n].astype(F32) + other[n].astype(F32)
         return (base.astype(F32) + normed(total, gain)).astype(BF)
 
-    ready(*THIRD)
-    psend_pick = pick(columns(flat("p_send")), mrows)
-    pslot_pick = pick(columns(flat("p_slot")), shards * cap_h)
-    precv_pick = pick2(columns(flat("p_recv")))
-    first = finish(mesh_ref[...], flat("g_recv"), hid, e_ow, flat("e_g"), 0)
+    first = finish(mesh_ref[...], g_onto, hid, e_ow, flat("e_g"), 0)
 
     mproj = dot(first, p_sw[...]).astype(BF)
     pbuf[...] = dot(psend_pick, mproj).astype(BF).reshape(pbuf.shape)
@@ -266,7 +269,7 @@
         proc_arrival(o).wait_recv()
     pre = dot(pslot_pick, precv[...].reshape(shards * cap_h, dh)) + pterm
     hid2[...] = silu(pre).astype(BF)
-    last = finish(first, flat("p_recv"), hid2, p_ow, flat("p_g"), 1)
+    last = finish(first, p_onto, hid2, p_ow, flat("p_g"), 1)
     mesh_out[...] = last
 
     projected = dot(last, d_sw[...]).astype(BF)

time: 39.5 us -> 39.5 us (level)
  no operation moved by 1% of the time
where the time goes in v5:
time: 39.5 us; the launch traced here: 39.3 us
  Pallas kernels  36.1 us (91%)
  local copies, waits for them, and re-layouts  2.53 us (6%)
  between operations  0.66 us (2%)
    pallas_call x1, Pallas kernels, per_device(): pl.pallas_call(functools.partial(kernel, nb, nm, cap_g, cap_h, cap_m), ou...  36.1 us
    unnamed x4, local copies, waits for them, and re-layouts  2.53 us

profile of v5, /device:TPU:0, one launch (start us, length us, event | category | flops | bytes accessed | tf_op | source)
XLA Modules:
  0.0 39.3 jit_solution(1414332271385255355)
XLA Ops:
  0.6 36.1 %shard_map.248 = (bf16[512,512]{1,0:T(8,128)(2,1)}, bf16[64,512]{1,0:T(8,128)(2,1)}) custom-call(bf16[1024,512]{1,0:T(8,128)(2,1)} %refs_0_.1, bf16[64,512]{1,0:T(8,128)(2,1)} %refs_1_.1, s32[1536]{0:T(1024)} %refs_2_.1, s32[1536]{0:T(1024)} %refs_3_.1, s32[1536]{0:T(1024)} %refs_4_.1, bf16[512,256]{1,0:T(8,128)(2,1)} %refs_5_.1, bf16[512,256]{1,0:T(8,128)(2,1)} %refs_6_.1, ...), custom_call_target="tpu_custom_call" | custom-call | tf_op jit(solution)/shard_map/pallas_call | solution.py:363
  36.8 0.0 copy-start
  36.8 1.9 %copy.29 = bf16[512,512]{1,0:T(8,128)(2,1)} copy(bf16[512,512]{1,0:T(8,128)(2,1)} %get-tuple-element.4) | data formatting | bytes 1048576
  38.7 0.0 copy-done
  38.7 0.6 %copy.30 = bf16[64,512]{1,0:T(8,128)(2,1)} copy(bf16[64,512]{1,0:T(8,128)(2,1)S(1)} %copy-done) | data formatting | bytes 131072
Async XLA Ops:
  36.8 1.9 %copy-start = (bf16[64,512]{1,0:T(8,128)(2,1)S(1)}, bf16[64,512]{1,0:T(8,128)(2,1)}, u32[]{:S(2)}) copy-start(bf16[64,512]{1,0:T(8,128)(2,1)} %get-tuple-element.5) | copy-start | bytes 196612
